TPU v7x, 512 devices: a whole 4x4x16 slice. The times are simulated.
512 devices in a mesh: grp: 16 (over x, y), trn: 32 (over z, core).
Axes of the slice: x: 4, y: 4, z: 16, core: 2. Of those that a mesh axis runs over, the one named last changes fastest.
Arguments:
- features: bfloat16 [131072, 1024], P(('grp', 'trn')), may hold values from -24 to 24
- query_rows: bfloat16 [131072, 512], P(('grp', 'trn')), may hold values from -6 to 6
- key_rows: bfloat16 [131072, 512], P(('grp', 'trn')), may hold values from -6 to 6
- w_value: bfloat16 [1024, 512], P(('grp', 'trn')), may hold values from -0.1875 to 0.1875
- cotangent: bfloat16 [131072, 512], P(('grp', 'trn')), may hold values from -6 to 6
- station: int32 [131072], P(('grp', 'trn')), may hold values from 47 to 8191, as said below
- bucket: int32 [131072], P(('grp', 'trn')), may hold values from 0 to 15
- slot_index: int32 [131072], P(('grp', 'trn')), may hold values from 0 to 8191, as said below
Outputs:
- mixed_out: bfloat16 [131072, 512], P(('grp', 'trn'))
- grad_features: bfloat16 [131072, 1024], P(('grp', 'trn'))
- grad_query: bfloat16 [131072, 512], P(('grp', 'trn'))
- grad_key: bfloat16 [131072, 512], P(('grp', 'trn'))
- grad_weight: float32 [1024, 512], P(('grp', 'trn'))
Inputs may be any that keep to these rules, and one draw needn't show every extreme that they name: Within each group of 8192 consecutive rows, slot_index is a permutation of the group's positions; of the rows of one device exactly 8 fall in each block of 256 consecutive positions. Along each group's station-major order, the rows of one station are consecutive, 1 to 48 of them, one station exactly 48; a station's id is the station-major position of its last row.
All inputs are finite; a program needn't handle non-finite values.
Results may differ from a plain program's by a relative error of at most 0.018.
Values may be sent and summed in bfloat16 or wider, within the bound.
A program may use at most 64 MiB of HBM per device.

v0:
```python
import jax
import jax.numpy as jnp
from jax import lax
from jax.sharding import PartitionSpec as P

HEADS = 8
HDIM = 64
S = 256
WIN = 128


def attend(query_part, key_part, value_part, allowed, factor):
    scores = (
        jnp.einsum("blhd,bmhd->bhlm", query_part, key_part, preferred_element_type=jnp.float32)
        * factor
    )
    scores = jnp.where(allowed[:, None], scores, -1e30)
    top_score = jnp.max(scores, -1, keepdims=True)
    raised = jnp.exp(scores - top_score)
    weights = raised / jnp.sum(raised, -1, keepdims=True)
    weights_half = weights.astype(jnp.bfloat16)
    output = jnp.einsum(
        "bhlm,bmhd->blhd", weights_half, value_part, preferred_element_type=jnp.float32
    )
    return (output.astype(jnp.bfloat16), weights, weights_half)


def attend_back(query_part, key_part, value_part, weights, weights_half, grad_out, factor):
    grad_weights = jnp.einsum(
        "blhd,bmhd->bhlm", grad_out, value_part, preferred_element_type=jnp.float32
    )
    row_dot = jnp.sum(weights * grad_weights, -1, keepdims=True)
    grad_scores = (weights * (grad_weights - row_dot) * factor).astype(jnp.bfloat16)
    grad_query = jnp.einsum(
        "bhlm,bmhd->blhd", grad_scores, key_part, preferred_element_type=jnp.float32
    )
    grad_key = jnp.einsum(
        "bhlm,blhd->bmhd", grad_scores, query_part, preferred_element_type=jnp.float32
    )
    grad_value = jnp.einsum(
        "bhlm,blhd->bmhd", weights_half, grad_out, preferred_element_type=jnp.float32
    )
    return (grad_query, grad_key, grad_value)


def shards(features, query_rows, key_rows, w_value, cotangent, station, bucket, slot_index):
    local_rows = features.shape[0]
    width = query_rows.shape[1]
    factor = HDIM ** (-0.5)
    members = lax.axis_size("trn")
    total_rows = local_rows * lax.axis_size("grp") * members
    counter = jnp.arange(local_rows, dtype=jnp.int32)
    order = jnp.argsort(slot_index // local_rows * local_rows + counter)
    restore = jnp.argsort(order)
    place, station_recv, bucket_recv = (
        lax.all_to_all(
            (slot_index % local_rows)[order], "trn", split_axis=0, concat_axis=0, tiled=True
        ),
        lax.all_to_all(station[order], "trn", split_axis=0, concat_axis=0, tiled=True),
        lax.all_to_all(bucket[order], "trn", split_axis=0, concat_axis=0, tiled=True),
    )
    arrange = jnp.argsort(place)
    station_major = station_recv[arrange].reshape(local_rows // WIN, WIN)
    bucket_major = bucket_recv[arrange].reshape(local_rows // WIN, WIN)
    window_mask = (station_major[:, :, None] == station_major[:, None, :]) & (
        bucket_major[:, None, :] <= bucket_major[:, :, None]
    )
    causal = jnp.broadcast_to(jnp.tril(jnp.ones((S, S), dtype=jnp.bool_)), (local_rows // S, S, S))

    def by_train(array):
        return array.reshape(local_rows // S, S, HEADS, HDIM)

    def by_window(array):
        return array.reshape(local_rows // WIN, WIN, HEADS, HDIM)

    def flatten(array):
        return array.reshape(local_rows, width)

    w_full = lax.all_gather(w_value, ("grp", "trn"), axis=0, tiled=True)
    values = jnp.dot(features, w_full, preferred_element_type=jnp.float32).astype(jnp.bfloat16)
    context, stop_weights, stop_half = attend(
        by_train(query_rows), by_train(key_rows), by_train(values), causal, factor
    )
    context = flatten(context)
    cot_send = cotangent[order]
    payload = (query_rows[order], key_rows[order], context[order])
    moved = (
        lax.all_to_all(payload[0], "trn", split_axis=0, concat_axis=0, tiled=True),
        lax.all_to_all(payload[1], "trn", split_axis=0, concat_axis=0, tiled=True),
        lax.all_to_all(payload[2], "trn", split_axis=0, concat_axis=0, tiled=True),
    )
    query_major = moved[0][arrange]
    key_major = moved[1][arrange]
    context_major = moved[2][arrange]
    mixed, window_weights, window_half = attend(
        by_window(query_major), by_window(key_major), by_window(context_major), window_mask, factor
    )
    mixed_send = flatten(mixed)[place]
    mixed_back = lax.all_to_all(mixed_send, "trn", split_axis=0, concat_axis=0, tiled=True)
    cot_recv = lax.all_to_all(cot_send, "trn", split_axis=0, concat_axis=0, tiled=True)
    mixed_out = mixed_back[restore]
    grad_major = cot_recv[arrange]
    win_query, win_key, win_context = attend_back(
        by_window(query_major),
        by_window(key_major),
        by_window(context_major),
        window_weights,
        window_half,
        by_window(grad_major),
        factor,
    )
    returned = (
        lax.all_to_all(
            flatten(win_query.astype(jnp.bfloat16))[place],
            "trn",
            split_axis=0,
            concat_axis=0,
            tiled=True,
        ),
        lax.all_to_all(
            flatten(win_key.astype(jnp.bfloat16))[place],
            "trn",
            split_axis=0,
            concat_axis=0,
            tiled=True,
        ),
        lax.all_to_all(
            flatten(win_context.astype(jnp.bfloat16))[place],
            "trn",
            split_axis=0,
            concat_axis=0,
            tiled=True,
        ),
    )
    query_back = returned[0][restore]
    key_back = returned[1][restore]
    grad_context = returned[2][restore]
    stop_query, stop_key, stop_value = attend_back(
        by_train(query_rows),
        by_train(key_rows),
        by_train(values),
        stop_weights,
        stop_half,
        by_train(grad_context),
        factor,
    )
    grad_value = flatten(stop_value).astype(jnp.bfloat16)
    grad_query = (flatten(stop_query) + query_back.astype(jnp.float32)).astype(jnp.bfloat16)
    grad_key = (flatten(stop_key) + key_back.astype(jnp.float32)).astype(jnp.bfloat16)
    grad_features = lax.dot_general(
        grad_value, w_full, (((1,), (1,)), ((), ())), preferred_element_type=jnp.float32
    ).astype(jnp.bfloat16)
    partial_grad = lax.dot_general(
        features, grad_value, (((0,), (0,)), ((), ())), preferred_element_type=jnp.float32
    )
    summed = lax.psum_scatter(partial_grad, ("grp", "trn"), scatter_dimension=0, tiled=True)
    grad_weight = summed * total_rows ** (-0.5)
    return (mixed_out, grad_features, grad_query, grad_key, grad_weight)


def solution(mesh):
    placed = (
        P(("grp", "trn"), None),
        P(("grp", "trn"), None),
        P(("grp", "trn"), None),
        P(("grp", "trn"), None),
        P(("grp", "trn"), None),
        P(("grp", "trn")),
        P(("grp", "trn")),
        P(("grp", "trn")),
    )
    return jax.shard_map(
        shards,
        mesh=mesh,
        in_specs=placed,
        out_specs=(
            P(("grp", "trn"), None),
            P(("grp", "trn"), None),
            P(("grp", "trn"), None),
            P(("grp", "trn"), None),
            P(("grp", "trn"), None),
        ),
        check_vma=False,
    )
```

profile of v0, /device:TPU:1, one launch (start us, length us, event | category | flops | bytes accessed | tf_op | source)
XLA Modules:
  0.0 849.2 jit_solution(13383835882384912854)
XLA Ops:
  8.0 3.2 sort.45
  11.1 2.0 gather_fusion.3
  13.8 16.7 %all-to-all-start.2 = ((s32[32,8,1]{1,2,0:T(1,128)}), s32[32,8,1]{1,2,0:T(1,128)S(1)}, u32[]{:S(2)}, u32[]{:S(2)}) async-start(s32[32,8,1]{1,2,0:T(1,128)} %bitcast.10), calls=%async_computation.2 | async-start | bytes 32768 | tf_op jit(solution)/shard_map/all_to_all | solution.py:59
  30.6 2.0 gather_fusion.5
  33.3 9.0 %all-to-all-done.2 = s32[32,8,1]{1,2,0:T(1,128)S(1)} async-done(((s32[32,8,1]{1,2,0:T(1,128)}), s32[32,8,1]{1,2,0:T(1,128)S(1)}, u32[]{:S(2)}, u32[]{:S(2)}) %all-to-all-start.2) | async-done | bytes 1056 | tf_op jit(solution)/shard_map/all_to_all | solution.py:59
  42.3 4.4 all-to-all-start.3
  46.7 1.9 gather_fusion.1
  49.3 9.2 %all-to-all-done.3 = s32[32,8,1]{1,2,0:T(1,128)S(1)} async-done(((s32[32,8,1]{1,2,0:T(1,128)}), s32[32,8,1]{1,2,0:T(1,128)S(1)}, u32[]{:S(2)}, u32[]{:S(2)}) %all-to-all-start.3) | async-done | bytes 1056 | tf_op jit(solution)/shard_map/all_to_all | solution.py:60
  58.5 4.4 all-to-all-start.1
  62.9 1.9 gather_fusion.13
  64.7 9.9 %all-to-all-done.1 = s32[32,8,1]{1,2,0:T(1,128)S(1)} async-done(((s32[32,8,1]{1,2,0:T(1,128)}), s32[32,8,1]{1,2,0:T(1,128)S(1)}, u32[]{:S(2)}, u32[]{:S(2)}) %all-to-all-start.1) | async-done | bytes 1056 | tf_op jit(solution)/shard_map/all_to_all | solution.py:56
  74.7 4.4 all-to-all-start.7
  79.8 1.9 gather_fusion.9
  81.7 19.4 %all-to-all-done.7 = bf16[32,8,512]{2,1,0:T(8,128)(2,1)S(1)} async-done(((bf16[32,8,512]{2,1,0:T(8,128)(2,1)}), bf16[32,8,512]{2,1,0:T(8,128)(2,1)S(1)}, u32[]{:S(2)}, u32[]{:S(2)}) %all-to-all-start.7) | async-done | bytes 262176 | tf_op jit(solution)/shard_map/all_to_all | solution.py:100
  101.1 4.7 all-to-all-start.5
  105.8 1.9 gather_fusion.7
  108.0 19.9 %all-to-all-done.5 = bf16[32,8,512]{2,1,0:T(8,128)(2,1)S(1)} async-done(((bf16[32,8,512]{2,1,0:T(8,128)(2,1)}), bf16[32,8,512]{2,1,0:T(8,128)(2,1)S(1)}, u32[]{:S(2)}, u32[]{:S(2)}) %all-to-all-start.5) | async-done | bytes 262176 | tf_op jit(solution)/shard_map/all_to_all | solution.py:89
  127.9 4.7 all-to-all-start.4
  132.6 2.2 fusion.55
  137.8 3.2 sort.46
  140.9 1.9 gather_fusion.6
  142.9 1.9 gather_fusion.4
  144.8 110.3 %all-gather.3.cloned.1.call-done = bf16[512,2,512]{2,1,0:T(2,128)(2,1)} async-done(((bf16[1,2,512]{2,1,0:T(2,128)(2,1)}), bf16[512,2,512]{2,1,0:T(2,128)(2,1)}) %all-gather.3.cloned.1.call-update) | async-done | bytes 1048592 | tf_op jit(solution)/shard_map/all_gather | solution.py:79
  257.3 2.0 convolution_convert_fusion.6
  259.4 1.9 gather_fusion
  261.3 6.9 all-to-all-start
  276.7 1.9 gather_fusion.15
  278.6 11.7 %all-to-all-done = bf16[32,8,512]{2,1,0:T(8,128)(2,1)S(1)} async-done(((bf16[32,8,512]{2,1,0:T(8,128)(2,1)}), bf16[32,8,512]{2,1,0:T(8,128)(2,1)S(1)}, u32[]{:S(2)}, u32[]{:S(2)}) %all-to-all-start) | async-done | bytes 262176 | tf_op jit(solution)/shard_map/all_to_all | solution.py:90
  290.2 4.5 all-to-all-start.8
  299.5 1.9 gather_fusion.11
  301.4 15.4 %all-to-all-done.8 = bf16[32,8,512]{2,1,0:T(8,128)(2,1)S(1)} async-done(((bf16[32,8,512]{2,1,0:T(8,128)(2,1)}), bf16[32,8,512]{2,1,0:T(8,128)(2,1)S(1)}, u32[]{:S(2)}, u32[]{:S(2)}) %all-to-all-start.8) | async-done | bytes 262176 | tf_op jit(solution)/shard_map/all_to_all | solution.py:127
  316.8 4.7 all-to-all-start.6
  321.5 3.2 sort.47
  326.9 2.2 fusion.24
  329.8 1.9 gather_fusion.19
  331.6 11.8 %all-to-all-done.6 = bf16[32,8,512]{2,1,0:T(8,128)(2,1)S(1)} async-done(((bf16[32,8,512]{2,1,0:T(8,128)(2,1)}), bf16[32,8,512]{2,1,0:T(8,128)(2,1)S(1)}, u32[]{:S(2)}, u32[]{:S(2)}) %all-to-all-start.6) | async-done | bytes 262176 | tf_op jit(solution)/shard_map/all_to_all | solution.py:99
  343.5 4.6 all-to-all-start.10
  349.5 2.0 convolution_convert_fusion.3
  353.4 3.4 fusion.23
  358.4 1.9 gather_fusion.17
  360.3 9.9 %all-to-all-done.10 = bf16[32,8,512]{2,1,0:T(8,128)(2,1)S(1)} async-done(((bf16[32,8,512]{2,1,0:T(8,128)(2,1)}), bf16[32,8,512]{2,1,0:T(8,128)(2,1)S(1)}, u32[]{:S(2)}, u32[]{:S(2)}) %all-to-all-start.10) | async-done | bytes 262176 | tf_op jit(solution)/shard_map/all_to_all | solution.py:120
  370.1 4.7 all-to-all-start.9
  374.8 1.8 fusion.57
  376.6 4.2 fusion.9
  381.1 5.1 fusion.12
  387.4 2.2 convolution_convert_fusion
  389.7 445.2 %all-reduce.3.cloned.1.call-done = f32[1024,512]{0,1:T(8,128)} async-done(((f32[1024,512]{0,1:T(8,128)}), f32[1024,512]{0,1:T(8,128)}) %all-reduce.3.cloned.1.call-update) | async-done | bytes 2097168
  836.6 1.9 gather_fusion.12
  (106 shorter events, 36.9 us)
Async XLA Ops:
  7.2 249.5 %copy-start = (bf16[256,1024]{1,0:T(8,128)(2,1)S(1)}, bf16[256,1024]{1,0:T(8,128)(2,1)}, u32[]{:S(2)}) copy-start(bf16[256,1024]{1,0:T(8,128)(2,1)} %param.8) | copy-start | bytes 1572868
  7.2 55.7 %copy-start.3 = (bf16[256,512]{1,0:T(8,128)(2,1)S(1)}, bf16[256,512]{1,0:T(8,128)(2,1)}, u32[]{:S(2)}) copy-start(bf16[256,512]{1,0:T(8,128)(2,1)} %param.12) | copy-start | bytes 786436
  13.8 28.5 %all-to-all-start.2 = ((s32[32,8,1]{1,2,0:T(1,128)}), s32[32,8,1]{1,2,0:T(1,128)S(1)}, u32[]{:S(2)}, u32[]{:S(2)}) async-start(s32[32,8,1]{1,2,0:T(1,128)} %bitcast.10), calls=%async_computation.2 | async-start | bytes 32768 | tf_op jit(solution)/shard_map/all_to_all | solution.py:59
  32.6 47.3 %copy-start.2 = (bf16[256,512]{1,0:T(8,128)(2,1)S(1)}, bf16[256,512]{1,0:T(8,128)(2,1)}, u32[]{:S(2)}) copy-start(bf16[256,512]{1,0:T(8,128)(2,1)} %param.10) | copy-start | bytes 786436
  42.3 16.2 %all-to-all-start.3 = ((s32[32,8,1]{1,2,0:T(1,128)}), s32[32,8,1]{1,2,0:T(1,128)S(1)}, u32[]{:S(2)}, u32[]{:S(2)}) async-start(s32[32,8,1]{1,2,0:T(1,128)} %bitcast.12), calls=%async_computation.3 | async-start | bytes 32768 | tf_op jit(solution)/shard_map/all_to_all | solution.py:60
  58.5 16.2 %all-to-all-start.1 = ((s32[32,8,1]{1,2,0:T(1,128)}), s32[32,8,1]{1,2,0:T(1,128)S(1)}, u32[]{:S(2)}, u32[]{:S(2)}) async-start(s32[32,8,1]{1,2,0:T(1,128)} %bitcast.9), calls=%async_computation.1 | async-start | bytes 32768 | tf_op jit(solution)/shard_map/all_to_all | solution.py:56
  64.7 41.0 %copy-start.1 = (bf16[256,512]{1,0:T(8,128)(2,1)S(1)}, bf16[256,512]{1,0:T(8,128)(2,1)}, u32[]{:S(2)}) copy-start(bf16[256,512]{1,0:T(8,128)(2,1)} %param.9) | copy-start | bytes 786436
  74.7 26.4 %all-to-all-start.7 = ((bf16[32,8,512]{2,1,0:T(8,128)(2,1)}), bf16[32,8,512]{2,1,0:T(8,128)(2,1)S(1)}, u32[]{:S(2)}, u32[]{:S(2)}) async-start(bf16[32,8,512]{2,1,0:T(8,128)(2,1)} %bitcast.22), calls=%async_computation.7 | async-start | bytes 524288 | tf_op jit(solution)/shard_map/all_to_all | solution.py:100
  79.1 176.1 %all-gather.3.cloned.1.call-start = ((), (), s32[]{:S(2)}) async-start(), calls=%async_computation.11 | async-start | bytes 1050624 | tf_op jit(solution)/shard_map/all_gather | solution.py:79
  101.1 26.8 %all-to-all-start.5 = ((bf16[32,8,512]{2,1,0:T(8,128)(2,1)}), bf16[32,8,512]{2,1,0:T(8,128)(2,1)S(1)}, u32[]{:S(2)}, u32[]{:S(2)}) async-start(bf16[32,8,512]{2,1,0:T(8,128)(2,1)} %bitcast.16), calls=%async_computation.5 | async-start | bytes 524288 | tf_op jit(solution)/shard_map/all_to_all | solution.py:89
  107.8 27.0 %copy-start.15 = (bf16[256,512]{0,1:T(8,128)(2,1)}, bf16[256,512]{0,1:T(8,128)(2,1)S(1)}, u32[]{:S(2)}) copy-start(bf16[256,512]{0,1:T(8,128)(2,1)S(1)} %copy.78) | copy-start | bytes 786436
  107.9 26.8 %copy-start.14 = (bf16[256,512]{0,1:T(8,128)(2,1)}, bf16[256,512]{0,1:T(8,128)(2,1)S(1)}, u32[]{:S(2)}) copy-start(bf16[256,512]{0,1:T(8,128)(2,1)S(1)} %copy.79) | copy-start | bytes 786436
  127.9 133.4 %all-to-all-start.4 = ((bf16[32,8,512]{2,1,0:T(8,128)(2,1)}), bf16[32,8,512]{2,1,0:T(8,128)(2,1)S(1)}, u32[]{:S(2)}, u32[]{:S(2)}) async-start(bf16[32,8,512]{2,1,0:T(8,128)(2,1)} %bitcast.14), calls=%async_computation.4 | async-start | bytes 524288 | tf_op jit(solution)/shard_map/all_to_all | solution.py:88
  257.2 2.0 copy-start.4
  261.3 28.9 %all-to-all-start = ((bf16[32,8,512]{2,1,0:T(8,128)(2,1)}), bf16[32,8,512]{2,1,0:T(8,128)(2,1)S(1)}, u32[]{:S(2)}, u32[]{:S(2)}) async-start(bf16[32,8,512]{2,1,0:T(8,128)(2,1)} %bitcast.7), calls=%async_computation | async-start | bytes 524288 | tf_op jit(solution)/shard_map/all_to_all | solution.py:90
  270.2 5.1 copy-start.7
  272.0 25.3 %copy-start.10 = (bf16[2,128,8,64]{1,3,2,0:T(8,128)(2,1)}, bf16[2,128,8,64]{1,3,2,0:T(8,128)(2,1)S(1)}, u32[]{:S(2)}) copy-start(bf16[2,128,8,64]{1,3,2,0:T(8,128)(2,1)S(1)} %copy.89) | copy-start | bytes 786436
  273.7 1.5 copy-start.12
  290.2 26.5 %all-to-all-start.8 = ((bf16[32,8,512]{2,1,0:T(8,128)(2,1)}), bf16[32,8,512]{2,1,0:T(8,128)(2,1)S(1)}, u32[]{:S(2)}, u32[]{:S(2)}) async-start(bf16[32,8,512]{2,1,0:T(8,128)(2,1)} %bitcast.25), calls=%async_computation.8 | async-start | bytes 524288 | tf_op jit(solution)/shard_map/all_to_all | solution.py:127
  294.7 2.5 copy-start.13
  298.9 25.8 %copy-start.8 = (bf16[2,128,8,64]{1,3,2,0:T(8,128)(2,1)S(1)}, bf16[2,128,8,64]{1,3,2,0:T(8,128)(2,1)}, u32[]{:S(2)}) copy-start(bf16[2,128,8,64]{1,3,2,0:T(8,128)(2,1)} %copy-done.7) | copy-start | bytes 786436
  316.8 26.7 %all-to-all-start.6 = ((bf16[32,8,512]{2,1,0:T(8,128)(2,1)}), bf16[32,8,512]{2,1,0:T(8,128)(2,1)S(1)}, u32[]{:S(2)}, u32[]{:S(2)}) async-start(bf16[32,8,512]{2,1,0:T(8,128)(2,1)} %bitcast.20), calls=%async_computation.6 | async-start | bytes 524288 | tf_op jit(solution)/shard_map/all_to_all | solution.py:99
  325.9 1.0 copy-start.6
  343.5 26.7 %all-to-all-start.10 = ((bf16[32,8,512]{2,1,0:T(8,128)(2,1)}), bf16[32,8,512]{2,1,0:T(8,128)(2,1)S(1)}, u32[]{:S(2)}, u32[]{:S(2)}) async-start(bf16[32,8,512]{2,1,0:T(8,128)(2,1)} %bitcast.43), calls=%async_computation.10 | async-start | bytes 524288 | tf_op jit(solution)/shard_map/all_to_all | solution.py:120
  348.1 486.7 %all-reduce.3.cloned.1.call-start = ((), (), s32[]{:S(2)}) async-start(), calls=%async_computation.12 | async-start | bytes 4194304
  351.5 5.2 copy-start.9
  351.5 1.8 copy-start.11
  356.8 18.0 %copy-start.5 = (bf16[256,512]{0,1:T(8,128)(2,1)S(1)}, bf16[256,512]{0,1:T(8,128)(2,1)}, u32[]{:S(2)}) copy-start(bf16[256,512]{0,1:T(8,128)(2,1)} %copy-done.4) | copy-start | bytes 786436
  360.3 16.4 %copy-start.16 = (bf16[256,512]{0,1:T(8,128)(2,1)S(1)}, bf16[256,512]{0,1:T(8,128)(2,1)}, u32[]{:S(2)}) copy-start(bf16[256,512]{0,1:T(8,128)(2,1)} %copy-done.15) | copy-start | bytes 786436
  370.1 469.5 %all-to-all-start.9 = ((bf16[32,8,512]{2,1,0:T(8,128)(2,1)}), bf16[32,8,512]{2,1,0:T(8,128)(2,1)S(1)}, u32[]{:S(2)}, u32[]{:S(2)}) async-start(bf16[32,8,512]{2,1,0:T(8,128)(2,1)} %bitcast.36), calls=%async_computation.9 | async-start | bytes 524288 | tf_op jit(solution)/shard_map/all_to_all | solution.py:113
Sparse Core Ops, SparseCore 0:
  84.5 170.6 all-gather.2
  354.3 480.4 all-reduce.2
where the time goes:
time: 850 us; the launch traced here: 849 us
  waiting for transfers between devices  672 us (79%)
  starting transfers between devices  64.8 us (8%)
  local copies, waits for them, and re-layouts  49.5 us (6%)
  matrix products  32.7 us (4%)
  other arithmetic  15.2 us (2%)
  between operations  14.6 us (2%)
    unnamed x3, waiting for transfers between devices  446 us
    all_gather x1, waiting for transfers between devices, shards(): w_full = lax.all_gather(w_value, ('grp', 'trn'), axis=0, tiled=True)  110 us
    all_to_all x1, waiting for transfers between devices, shards(): lax.all_to_all(payload[1], 'trn', split_axis=0, concat_axis=0, tiled=True)  19.9 us
    all_to_all x1, waiting for transfers between devices, shards(): lax.all_to_all(cot_send, 'trn', split_axis=0, concat_axis=0, tiled=True)  19.4 us
  transfers between devices with their start and end apart: 13, of which 11 were waited for; matrix products, arithmetic and copies ran while one was open for 10% of the time, Pallas kernels for 0%

commit v1 on v0

v1 whole, which is shorter than its diff:
```python
import functools

import jax
import jax.numpy as jnp
from jax import lax
from jax.experimental import pallas as pl
from jax.experimental.pallas import tpu as pltpu
from jax.sharding import PartitionSpec as P

MESH = pl.DeviceIdType.MESH
BF16 = jnp.bfloat16
F32 = jnp.float32
I32 = jnp.int32
HEADS = 8
HDIM = 64
HD = 512
D = 1024
R = 256
WIN = 128
MEMBERS = 32
GROUPS = 16
CHIPS = 16
NEG = -1e30


def dot(a, b):
    return lax.dot_general(a, b, (((1,), (0,)), ((), ())), preferred_element_type=F32)


def dot_nt(a, b):
    return lax.dot_general(a, b, (((1,), (1,)), ((), ())), preferred_element_type=F32)


def dot_tn(a, b):
    return lax.dot_general(a, b, (((0,), (0,)), ((), ())), preferred_element_type=F32)


def iota(shape, dim):
    return lax.broadcasted_iota(I32, shape, dim)


def to_col(row):
    eye = iota((R, R), 0) == iota((R, R), 1)
    return jnp.sum(jnp.where(eye, jnp.broadcast_to(row, (R, R)), 0), axis=1, keepdims=True)


def to_row(col):
    eye = iota((R, R), 0) == iota((R, R), 1)
    return jnp.sum(jnp.where(eye, jnp.broadcast_to(col, (R, R)), 0), axis=0, keepdims=True)


def pack(rows):
    cut = rows.reshape(MEMBERS, 8, HD)
    return jnp.concatenate([cut[:, :, : HD // 2], cut[:, :, HD // 2 :]], axis=1).reshape(2 * R, HD // 2).astype(BF16)


def unpack(block):
    cut = block.astype(F32).reshape(MEMBERS, 16, HD // 2)
    low = cut[:, :8].reshape(R, HD // 2)
    high = cut[:, 8:].reshape(R, HD // 2)
    return jnp.concatenate([low, high], axis=1).astype(BF16)


def softmax(scores):
    top = jnp.max(scores, axis=1, keepdims=True)
    raised = jnp.exp(scores - top)
    return raised * (1.0 / jnp.sum(raised, axis=1, keepdims=True))


def kernel(
    feat, query, key, w_part, cot, station, bucket, slot,
    mixed_o, gfeat_o, gq_o, gk_o, gw_o,
    order, restore, bias, stop_p, win_p,
    send_a, recv_a, send_m, recv_m, send_c, recv_c, send_d, recv_d, send_r, recv_r,
    w_send, w_recv, w_rows, w_full,
    vals, ctx, grad_c, grad_v, stop_q, stop_k,
    qw, kw, vw, dw, out_m, out_q, out_k,
    gw_own, rs0_send, rs0_recv, rs1_send, rs1_recv, rs2_send, rs2_recv, rs3_send, rs3_recv,
    sems,
):
    grp = lax.axis_index("grp")
    trn = lax.axis_index("trn")
    chip = trn // 2
    core = trn % 2
    sibling = chip * 2 + (1 - core)

    def member(step):
        return lax.rem(trn + step, MEMBERS)

    def group(step):
        return lax.rem(grp + step, GROUPS)

    barrier = pltpu.get_barrier_semaphore()

    @pl.loop(1, MEMBERS)
    def _(step):
        pl.semaphore_signal(barrier, inc=1, device_id=(grp, member(step)), device_id_type=MESH)

    @pl.loop(1, GROUPS)
    def _(step):
        pl.semaphore_signal(barrier, inc=1, device_id=(group(step), trn), device_id_type=MESH)

    def blocks(ref, who, rows):
        return ref.at[pl.ds(pl.multiple_of(who * rows, rows), rows)]

    def exchange(send, recv, rows, ssem, rsem):
        pltpu.make_async_copy(blocks(send, trn, rows), blocks(recv, trn, rows), sems.at[rsem]).start()

        @pl.loop(1, MEMBERS)
        def _(step):
            peer = member(step)
            pltpu.make_async_remote_copy(
                src_ref=blocks(send, peer, rows), dst_ref=blocks(recv, trn, rows),
                send_sem=sems.at[ssem], recv_sem=sems.at[rsem],
                device_id=(grp, peer), device_id_type=MESH,
            ).start()

    def wait_for(ref, sem):
        pltpu.make_async_copy(ref, ref, sems.at[sem]).wait()

    def arrived(recv, rsem):
        wait_for(recv, rsem)

    def sent(send, rows, ssem):
        wait_for(send.at[pl.ds(0, (MEMBERS - 1) * rows)], ssem)

    slot_row = slot[...]
    goal_row = slot_row // R
    goal_col = to_col(goal_row)
    same = (goal_col == goal_row) & (iota((R, R), 0) < iota((R, R), 1))
    rank_row = jnp.sum(jnp.where(same, 1, 0), axis=0, keepdims=True)
    pos_row = goal_row * 8 + rank_row
    pos_col = to_col(pos_row)
    picks = iota((R, R), 0) == pos_row
    order[...] = jnp.where(picks, 1.0, 0.0).astype(BF16)
    restore[...] = jnp.where(pos_col == iota((R, R), 1), 1.0, 0.0).astype(BF16)

    half = HD // 2
    send_a[:, 0:half] = pack(dot(order[...], query[...]))
    send_a[:, half : 2 * half] = pack(dot(order[...], key[...]))
    send_a[:, 2 * half :] = pack(dot(order[...], cot[...]))

    lane = iota((R, 128), 1)
    within = iota((R, 128), 0) % 8

    def sorted_col(row):
        return jnp.sum(jnp.where(picks, jnp.broadcast_to(row, (R, R)), 0), axis=1, keepdims=True)

    place_col = sorted_col(slot_row % R)
    station_col = sorted_col(station[...])
    bucket_col = sorted_col(bucket[...])
    meta = (
        jnp.where(lane == within, place_col, 0)
        + jnp.where(lane == within + 8, station_col, 0)
        + jnp.where(lane == within + 16, bucket_col, 0)
    )
    send_m[...] = jnp.sum(meta.reshape(MEMBERS, 8, 128), axis=1, keepdims=True)
    w_send[...] = w_part[...].astype(F32)

    pl.semaphore_wait(barrier, MEMBERS - 1 + GROUPS - 1)

    near = trn // 16
    index = lax.rem(trn, 16)
    own_near = core == near

    @pl.when(own_near)
    def _():
        pltpu.make_async_copy(w_send, w_recv.at[index], sems.at[1]).start()

    @pl.when(jnp.logical_not(own_near))
    def _():
        pltpu.make_async_remote_copy(
            src_ref=w_send, dst_ref=w_recv.at[index], send_sem=sems.at[0], recv_sem=sems.at[1],
            device_id=(grp, chip * 2 + near), device_id_type=MESH,
        ).start()

    @pl.loop(1, CHIPS)
    def _(step):
        pltpu.make_async_remote_copy(
            src_ref=w_send, dst_ref=w_recv.at[index], send_sem=sems.at[0], recv_sem=sems.at[1],
            device_id=(grp, lax.rem(chip + step, CHIPS) * 2 + near), device_id_type=MESH,
        ).start()

    def all_blocks_m(step):
        peer = member(step)
        pltpu.make_async_remote_copy(
            src_ref=send_m.at[peer], dst_ref=recv_m.at[trn], send_sem=sems.at[4], recv_sem=sems.at[5],
            device_id=(grp, peer), device_id_type=MESH,
        ).start()

    pltpu.make_async_copy(send_m.at[trn], recv_m.at[trn], sems.at[5]).start()
    pl.loop(1, MEMBERS)(all_blocks_m)
    exchange(send_a, recv_a, 16, 2, 3)

    arrived(w_recv, 1)
    for step in range(CHIPS):
        w_rows[2 * step : 2 * step + 2, :] = w_recv[step]
    w_full[grp, core] = w_rows[...].astype(BF16)

    @pl.loop(1, GROUPS)
    def _(step):
        pltpu.make_async_remote_copy(
            src_ref=w_full.at[grp, core], dst_ref=w_full.at[grp, core], send_sem=sems.at[6], recv_sem=sems.at[7],
            device_id=(group(step), trn), device_id_type=MESH,
        ).start()

    low_lane = iota((R, 128), 1) < HDIM

    def heads_of(ref, pair):
        part = ref[:, pl.ds(pl.multiple_of(pair * 128, 128), 128)]
        zero = jnp.zeros_like(part)
        return part, jnp.where(low_lane, part, zero), jnp.where(low_lane, zero, part)

    def cols(pair):
        return (slice(None), pl.ds(pl.multiple_of(pair * 128, 128), 128))

    def weights_into(target, q_ref, k_ref):
        @pl.loop(0, HEADS // 2)
        def _(pair):
            k_pair = k_ref[cols(pair)]
            _, *q_heads = heads_of(q_ref, pair)
            for head in range(2):
                scores = dot_nt(q_heads[head], k_pair) * (HDIM ** -0.5) + bias[...]
                target[2 * pair + head] = softmax(scores).astype(BF16)

    bias[...] = jnp.where(iota((R, R), 1) <= iota((R, R), 0), 0.0, NEG)
    weights_into(stop_p, query, key)

    wait_for(w_full.at[pl.ds(0, GROUPS - 1), core], 7)
    wait_for(w_full.at[pl.ds(0, GROUPS - 1), core], 6)
    swap_w = pltpu.make_async_remote_copy(
        src_ref=w_full.at[:, core], dst_ref=w_full.at[:, core], send_sem=sems.at[8], recv_sem=sems.at[9],
        device_id=(grp, sibling), device_id_type=MESH,
    )
    swap_w.start()
    swap_w.wait()

    weight = w_full[...].reshape(D, HD)
    vals[...] = dot(feat[...], weight).astype(BF16)

    def attend(p_ref, v_ref, out_ref):
        @pl.loop(0, HEADS // 2)
        def _(pair):
            v_pair = v_ref[cols(pair)]
            first = dot(p_ref[2 * pair], v_pair)
            second = dot(p_ref[2 * pair + 1], v_pair)
            out_ref[cols(pair)] = jnp.where(low_lane, first, second).astype(out_ref.dtype)

    def attend_value_back(p_ref, d_ref, out_ref):
        @pl.loop(0, HEADS // 2)
        def _(pair):
            d_pair = d_ref[cols(pair)]
            first = dot_tn(p_ref[2 * pair], d_pair)
            second = dot_tn(p_ref[2 * pair + 1], d_pair)
            out_ref[cols(pair)] = jnp.where(low_lane, first, second).astype(out_ref.dtype)

    def attend_back(p_ref, q_ref, k_ref, v_ref, d_ref, dq_ref, dk_ref):
        @pl.loop(0, HEADS // 2)
        def _(pair):
            q_pair, k_pair, v_pair = q_ref[cols(pair)], k_ref[cols(pair)], v_ref[cols(pair)]
            _, *d_heads = heads_of(d_ref, pair)
            dq, dk = [], []
            for head in range(2):
                weights = p_ref[2 * pair + head].astype(F32)
                grad = dot_nt(d_heads[head], v_pair)
                row_dot = jnp.sum(weights * grad, axis=1, keepdims=True)
                grad = (weights * (grad - row_dot)).astype(BF16)
                dq.append(dot(grad, k_pair))
                dk.append(dot_tn(grad, q_pair))
            factor = HDIM ** -0.5
            dq_ref[cols(pair)] = (jnp.where(low_lane, dq[0], dq[1]) * factor).astype(dq_ref.dtype)
            dk_ref[cols(pair)] = (jnp.where(low_lane, dk[0], dk[1]) * factor).astype(dk_ref.dtype)

    attend(stop_p, vals, ctx)
    send_c[...] = pack(dot(order[...], ctx[...]))
    exchange(send_c, recv_c, 16, 10, 11)

    arrived(recv_m, 5)
    got = jnp.broadcast_to(recv_m[...], (MEMBERS, 8, 128)).reshape(R, 128)

    def field(number):
        return jnp.sum(jnp.where(lane == within + 8 * number, got, 0), axis=1, keepdims=True)

    piece = field(1) * 2 + field(0) // WIN
    buckets = field(2)
    allowed = (piece == to_row(piece)) & (to_row(buckets) <= buckets)
    bias[...] = jnp.where(allowed, 0.0, NEG)
    arrived(recv_a, 3)
    qw[...] = unpack(recv_a[:, 0:half])
    kw[...] = unpack(recv_a[:, half : 2 * half])
    dw[...] = unpack(recv_a[:, 2 * half :])
    weights_into(win_p, qw, kw)
    attend_value_back(win_p, dw, out_m)
    send_d[...] = pack(out_m[...])
    exchange(send_d, recv_d, 16, 12, 13)

    arrived(recv_c, 11)
    vw[...] = unpack(recv_c[...])
    attend(win_p, vw, out_m)
    attend_back(win_p, qw, kw, vw, dw, out_q, out_k)
    send_r[:, 0:half] = pack(out_m[...])
    send_r[:, half : 2 * half] = pack(out_q[...])
    send_r[:, 2 * half :] = pack(out_k[...])
    exchange(send_r, recv_r, 16, 14, 15)

    def put_back(block):
        return dot(restore[...], unpack(block))

    arrived(recv_d, 13)
    grad_c[...] = put_back(recv_d[...]).astype(BF16)
    attend_value_back(stop_p, grad_c, grad_v)

    mine = (slice(None), pl.ds(pl.multiple_of(core * half, half), half))
    other = (slice(None), pl.ds(pl.multiple_of((1 - core) * half, half), half))
    rs0_send[...] = dot_tn(feat[...], grad_v[other]).astype(BF16)
    swap_0 = pltpu.make_async_remote_copy(
        src_ref=rs0_send, dst_ref=rs0_recv, send_sem=sems.at[16], recv_sem=sems.at[17],
        device_id=(grp, sibling), device_id_type=MESH,
    )
    swap_0.start()
    gw_own[...] = dot_tn(feat[...], grad_v[mine])
    swap_0.wait()
    rs1_send[...] = (gw_own[...] + rs0_recv[...].astype(F32)).astype(BF16).reshape(GROUPS, 64, half)
    rs1_recv[grp] = rs1_send[grp]

    @pl.loop(1, GROUPS)
    def _(step):
        peer = group(step)
        pltpu.make_async_remote_copy(
            src_ref=rs1_send.at[peer], dst_ref=rs1_recv.at[grp], send_sem=sems.at[18], recv_sem=sems.at[19],
            device_id=(peer, trn), device_id_type=MESH,
        ).start()

    attend_back(stop_p, query, key, vals, grad_c, stop_q, stop_k)

    wait_for(rs1_recv.at[pl.ds(0, GROUPS - 1)], 19)
    total = rs1_recv[0].astype(F32)
    for step in range(1, GROUPS):
        total = total + rs1_recv[step].astype(F32)
    for step in range(CHIPS):
        rs2_send[step] = total[4 * step : 4 * step + 4]
    rs2_recv[chip] = rs2_send[chip]

    @pl.loop(1, CHIPS)
    def _(step):
        peer = lax.rem(chip + step, CHIPS)
        pltpu.make_async_remote_copy(
            src_ref=rs2_send.at[peer], dst_ref=rs2_recv.at[chip], send_sem=sems.at[20], recv_sem=sems.at[21],
            device_id=(grp, peer * 2 + core), device_id_type=MESH,
        ).start()

    gfeat_o[...] = dot_nt(grad_v[...], w_full[...].reshape(D, HD)).astype(BF16)

    wait_for(rs2_recv.at[pl.ds(0, CHIPS - 1)], 21)
    mine_4 = rs2_recv[0]
    for step in range(1, CHIPS):
        mine_4 = mine_4 + rs2_recv[step]
    mine_4 = mine_4 * ((R * MEMBERS * GROUPS) ** -0.5)
    first, second = mine_4[0:2], mine_4[2:4]
    is_first = core == 0
    rs3_send[...] = jnp.where(is_first, second, first)
    swap_3 = pltpu.make_async_remote_copy(
        src_ref=rs3_send, dst_ref=rs3_recv, send_sem=sems.at[22], recv_sem=sems.at[23],
        device_id=(grp, sibling), device_id_type=MESH,
    )
    swap_3.start()
    kept = jnp.where(is_first, first, second)
    swap_3.wait()
    swapped = rs3_recv[...]
    gw_o[:, 0:half] = jnp.where(is_first, kept, swapped)
    gw_o[:, half:] = jnp.where(is_first, swapped, kept)

    arrived(recv_r, 15)
    mixed_o[...] = put_back(recv_r[:, 0:half]).astype(BF16)
    gq_o[...] = (stop_q[...] + put_back(recv_r[:, half : 2 * half])).astype(BF16)
    gk_o[...] = (stop_k[...] + put_back(recv_r[:, 2 * half :])).astype(BF16)

    sent(send_a, 16, 2)
    sent(send_m, 1, 4)
    sent(send_c, 16, 10)
    sent(send_d, 16, 12)
    sent(send_r, 16, 14)
    wait_for(w_recv.at[pl.ds(0, CHIPS - 1)], 0)

    @pl.when(jnp.logical_not(own_near))
    def _():
        wait_for(w_send, 0)

    wait_for(rs1_send.at[pl.ds(0, GROUPS - 1)], 18)
    wait_for(rs2_send.at[pl.ds(0, CHIPS - 1)], 20)


def shards(features, query_rows, key_rows, w_value, cotangent, station, bucket, slot_index):
    half = HD // 2
    vmem = pl.BlockSpec(memory_space=pltpu.VMEM)

    def buffer(shape, dtype):
        return pltpu.VMEM(shape, dtype)

    scratch = [
        buffer((R, R), BF16), buffer((R, R), BF16), buffer((R, R), F32),
        buffer((HEADS, R, R), BF16), buffer((HEADS, R, R), BF16),
        buffer((2 * R, 3 * half), BF16), buffer((2 * R, 3 * half), BF16),
        buffer((MEMBERS, 1, 128), I32), buffer((MEMBERS, 1, 128), I32),
        buffer((2 * R, half), BF16), buffer((2 * R, half), BF16),
        buffer((2 * R, half), BF16), buffer((2 * R, half), BF16),
        buffer((2 * R, 3 * half), BF16), buffer((2 * R, 3 * half), BF16),
        buffer((2, HD), F32), buffer((CHIPS, 2, HD), F32), buffer((32, HD), F32), buffer((GROUPS, 2, 32, HD), BF16),
        buffer((R, HD), BF16), buffer((R, HD), BF16), buffer((R, HD), BF16), buffer((R, HD), BF16),
        buffer((R, HD), F32), buffer((R, HD), F32),
        buffer((R, HD), BF16), buffer((R, HD), BF16), buffer((R, HD), BF16), buffer((R, HD), BF16),
        buffer((R, HD), F32), buffer((R, HD), F32), buffer((R, HD), F32),
        buffer((D, half), F32), buffer((D, half), BF16), buffer((D, half), BF16),
        buffer((GROUPS, 64, half), BF16), buffer((GROUPS, 64, half), BF16),
        buffer((CHIPS, 4, half), F32), buffer((CHIPS, 4, half), F32),
        buffer((2, half), F32), buffer((2, half), F32),
        pltpu.SemaphoreType.DMA((24,)),
    ]
    return pl.pallas_call(
        kernel,
        out_shape=(
            jax.ShapeDtypeStruct((R, HD), BF16),
            jax.ShapeDtypeStruct((R, D), BF16),
            jax.ShapeDtypeStruct((R, HD), BF16),
            jax.ShapeDtypeStruct((R, HD), BF16),
            jax.ShapeDtypeStruct((2, HD), F32),
        ),
        in_specs=[vmem] * 8,
        out_specs=(vmem,) * 5,
        scratch_shapes=scratch,
        compiler_params=pltpu.CompilerParams(
            collective_id=0, has_side_effects=True, vmem_limit_bytes=48 * 1024 * 1024
        ),
        name="delay_attention",
    )(
        features, query_rows, key_rows, w_value, cotangent,
        station.reshape(1, R), bucket.reshape(1, R), slot_index.reshape(1, R),
    )


def solution(mesh):
    rows = P(("grp", "trn"), None)
    ids = P(("grp", "trn"))
    return jax.shard_map(
        shards,
        mesh=mesh,
        in_specs=(rows,) * 5 + (ids,) * 3,
        out_specs=(rows,) * 5,
        check_vma=False,
    )
```

time: 850 us -> 128 us (0.15)
  waiting for transfers between devices: 672 us -> 0 us
  Pallas kernels: 0 us -> 119 us
  starting transfers between devices: 64.8 us -> 0 us
  local copies, waits for them, and re-layouts: 49.5 us -> 8.08 us
  matrix products: 32.7 us -> 0 us
  other arithmetic: 15.2 us -> 0 us
  between operations: 14.6 us -> 0.68 us
    unnamed x3 -> x0, waiting for transfers between devices: 446 us -> none
    pallas_call x0 -> x1, Pallas kernels: none -> 119 us  [shards(): pl.pallas_call(kernel, out_shape=(jax.ShapeDtypeStruct((R, HD), BF16), ja...]
    all_to_all x11 -> x0, waiting for transfers between devices: 116 us -> none  [the longest x1 19.9 us: shards(): lax.all_to_all(payload[1], 'trn', split_axis=0, concat_axis=0, tiled=True)]
    all_gather x1 -> x0, waiting for transfers between devices: 110 us -> none  [shards(): w_full = lax.all_gather(w_value, ('grp', 'trn'), axis=0, tiled=True)]
    all_to_all x11 -> x0, starting transfers between devices: 64.7 us -> none  [the longest x1 16.7 us: shards(): lax.all_to_all(station[order], 'trn', split_axis=0, concat_axis=0, tiled=...]
    gather x22 -> x0, local copies, waits for them, and re-layouts: 34.7 us -> none  [the longest x3 5.56 us: shards(): payload = (query_rows[order], key_rows[order], context[order])]
    dot_general x13 -> x0, matrix products: 29 us -> none  [the longest x2 8.5 us: attend_back(): jnp.einsum('bhlm,bmhd->blhd', grad_scores, key_part, preferred_element_ty...]
    sort x3 -> x0, other arithmetic: 9.5 us -> none  [the longest x1 3.17 us: shards(): order = jnp.argsort(slot_index // local_rows * local_rows + counter)]
  transfers between devices with their start and end apart: 13 -> 0, of which waited for: 11 -> 0; matrix products, arithmetic and copies ran while one was open for 10% -> 0% of each run, Pallas kernels for 0% -> 0%
where the time goes in v1:
time: 128 us
  Pallas kernels  119 us (93%)
  local copies, waits for them, and re-layouts  8.08 us (6%)
    pallas_call x1, Pallas kernels, shards(): pl.pallas_call(kernel, out_shape=(jax.ShapeDtypeStruct((R, HD), BF16), ja...  119 us
    unnamed x21, local copies, waits for them, and re-layouts  8.08 us

profile of v1, /device:TPU:1, one launch (start us, length us, event | category | flops | bytes accessed | tf_op | source)
XLA Modules:
  0.0 128.2 jit_solution(8985709368561803010)
XLA Ops:
  0.6 0.0 copy-start.6
  0.6 0.0 copy-start.7
  0.7 0.0 copy-start.4
  0.7 0.0 copy-start.5
  0.7 0.6 copy-done.6
  1.3 0.0 copy-done.7
  1.3 0.0 copy-done.4
  1.3 0.0 copy-done.5
  1.4 0.0 copy-start
  1.4 1.0 copy-done
  2.4 0.0 copy-start.1
  2.4 0.9 copy-done.1
  3.4 0.0 copy-start.2
  3.4 0.9 copy-done.2
  4.3 0.0 copy-start.3
  4.3 0.9 copy-done.3
  5.3 119.4 %delay_attention.1 = (bf16[256,512]{1,0:T(8,128)(2,1)S(1)}, bf16[256,1024]{1,0:T(8,128)(2,1)S(1)}, bf16[256,512]{1,0:T(8,128)(2,1)S(1)}, bf16[256,512]{1,0:T(8,128)(2,1)S(1)}, f32[2,512]{1,0:T(2,128)S(1)}) custom-call(bf16[256,1024]{1,0:T(8,128)(2,1)S(1)} %copy-done, bf16[256,512]{1,0:T(8,128)(2,1)S(1)} %copy-done.1, bf16[256,512]{1,0:T(8,128)(2,1)S(1)} %copy-done.2, ...), custom_call_target="tpu_custom_call" | custom-call | tf_op jit(solution)/shard_map/delay_attention/pallas_call | solution.py:419
  124.7 0.7 copy.18
  125.4 0.8 copy.19
  126.2 0.7 copy.20
  126.9 0.7 copy.21
  127.6 0.6 copy.22
Async XLA Ops:
  0.6 0.7 copy-start.6
  0.6 0.7 copy-start.7
  0.7 0.7 copy-start.4
  0.7 0.7 copy-start.5
  1.4 1.0 copy-start
  2.4 0.9 copy-start.1
  3.4 0.9 copy-start.2
  4.3 0.9 copy-start.3

commit v2 on v1

--- a/solution.py
+++ b/solution.py
@@ -68,16 +68,27 @@
 
 
 def kernel(
+    feat_in, query_in, key_in, w_in, cot_in, station_in, bucket_in, slot_in,
+    mixed_o, gfeat_o, gq_o, gk_o, gw_o,
     feat, query, key, w_part, cot, station, bucket, slot,
-    mixed_o, gfeat_o, gq_o, gk_o, gw_o,
     order, restore, bias, stop_p, win_p,
-    send_a, recv_a, send_m, recv_m, send_c, recv_c, send_d, recv_d, send_r, recv_r,
+    send, recv, send_m, recv_m,
     w_send, w_recv, w_rows, w_full,
     vals, ctx, grad_c, grad_v, stop_q, stop_k,
     qw, kw, vw, dw, out_m, out_q, out_k,
-    gw_own, rs0_send, rs0_recv, rs1_send, rs1_recv, rs2_send, rs2_recv, rs3_send, rs3_recv,
-    sems,
+    gw_own, rs0_send, rs0_recv, rs1_send, rs1_recv, rs1_sum, rs2_swap, rs2_rows, rs2_send, rs2_recv,
+    rs3_rows, rs3_send, rs3_recv,
+    sems, in_sems, send_sems, recv_sems,
 ):
+    copies_in = [
+        pltpu.make_async_copy(source, target, in_sems.at[number])
+        for number, (source, target) in enumerate((
+            (slot_in, slot), (query_in, query), (w_in, w_part), (station_in, station), (bucket_in, bucket),
+            (key_in, key), (cot_in, cot), (feat_in, feat),
+        ))
+    ]
+    for copy in copies_in:
+        copy.start()
     grp = lax.axis_index("grp")
     trn = lax.axis_index("trn")
     chip = trn // 2
@@ -100,30 +111,32 @@
     def _(step):
         pl.semaphore_signal(barrier, inc=1, device_id=(group(step), trn), device_id_type=MESH)
 
-    def blocks(ref, who, rows):
-        return ref.at[pl.ds(pl.multiple_of(who * rows, rows), rows)]
-
-    def exchange(send, recv, rows, ssem, rsem):
-        pltpu.make_async_copy(blocks(send, trn, rows), blocks(recv, trn, rows), sems.at[rsem]).start()
+    def block(number, ref, who):
+        return ref.at[number, pl.ds(pl.multiple_of(who * 16, 16), 16)]
+
+    def exchange(number):
+        pltpu.make_async_copy(block(number, send, trn), block(number, recv, trn), recv_sems.at[number]).start()
 
         @pl.loop(1, MEMBERS)
         def _(step):
             peer = member(step)
             pltpu.make_async_remote_copy(
-                src_ref=blocks(send, peer, rows), dst_ref=blocks(recv, trn, rows),
-                send_sem=sems.at[ssem], recv_sem=sems.at[rsem],
+                src_ref=block(number, send, peer), dst_ref=block(number, recv, trn),
+                send_sem=send_sems.at[number], recv_sem=recv_sems.at[number],
                 device_id=(grp, peer), device_id_type=MESH,
             ).start()
 
     def wait_for(ref, sem):
         pltpu.make_async_copy(ref, ref, sems.at[sem]).wait()
 
-    def arrived(recv, rsem):
-        wait_for(recv, rsem)
-
-    def sent(send, rows, ssem):
-        wait_for(send.at[pl.ds(0, (MEMBERS - 1) * rows)], ssem)
-
+    def arrived(number):
+        pltpu.make_async_copy(recv.at[number], recv.at[number], recv_sems.at[number]).wait()
+
+    def sent(number):
+        blocks = send.at[number, pl.ds(0, (MEMBERS - 1) * 16)]
+        pltpu.make_async_copy(blocks, blocks, send_sems.at[number]).wait()
+
+    copies_in[0].wait()
     slot_row = slot[...]
     goal_row = slot_row // R
     goal_col = to_col(goal_row)
@@ -133,13 +146,44 @@
     pos_col = to_col(pos_row)
     picks = iota((R, R), 0) == pos_row
     order[...] = jnp.where(picks, 1.0, 0.0).astype(BF16)
-    restore[...] = jnp.where(pos_col == iota((R, R), 1), 1.0, 0.0).astype(BF16)
 
     half = HD // 2
-    send_a[:, 0:half] = pack(dot(order[...], query[...]))
-    send_a[:, half : 2 * half] = pack(dot(order[...], key[...]))
-    send_a[:, 2 * half :] = pack(dot(order[...], cot[...]))
-
+    copies_in[1].wait()
+    send[0] = pack(dot(order[...], query[...]))
+    copies_in[2].wait()
+    w_send[...] = w_part[...].astype(F32)
+
+    pl.semaphore_wait(barrier, MEMBERS - 1 + GROUPS - 1)
+
+    near = trn // 16
+    index = lax.rem(trn, 16)
+    own_near = core == near
+
+    @pl.when(own_near)
+    def _():
+        pltpu.make_async_copy(w_send, w_recv.at[index], sems.at[1]).start()
+
+    @pl.when(jnp.logical_not(own_near))
+    def _():
+        pltpu.make_async_remote_copy(
+            src_ref=w_send, dst_ref=w_recv.at[index], send_sem=sems.at[0], recv_sem=sems.at[1],
+            device_id=(grp, chip * 2 + near), device_id_type=MESH,
+        ).start()
+
+    @pl.loop(1, CHIPS)
+    def _(step):
+        pltpu.make_async_remote_copy(
+            src_ref=w_send, dst_ref=w_recv.at[index], send_sem=sems.at[0], recv_sem=sems.at[1],
+            device_id=(grp, lax.rem(chip + step, CHIPS) * 2 + near), device_id_type=MESH,
+        ).start()
+
+    exchange(0)
+    copies_in[5].wait()
+    send[1] = pack(dot(order[...], key[...]))
+    exchange(1)
+
+    copies_in[3].wait()
+    copies_in[4].wait()
     lane = iota((R, 128), 1)
     within = iota((R, 128), 0) % 8
 
@@ -155,31 +199,6 @@
         + jnp.where(lane == within + 16, bucket_col, 0)
     )
     send_m[...] = jnp.sum(meta.reshape(MEMBERS, 8, 128), axis=1, keepdims=True)
-    w_send[...] = w_part[...].astype(F32)
-
-    pl.semaphore_wait(barrier, MEMBERS - 1 + GROUPS - 1)
-
-    near = trn // 16
-    index = lax.rem(trn, 16)
-    own_near = core == near
-
-    @pl.when(own_near)
-    def _():
-        pltpu.make_async_copy(w_send, w_recv.at[index], sems.at[1]).start()
-
-    @pl.when(jnp.logical_not(own_near))
-    def _():
-        pltpu.make_async_remote_copy(
-            src_ref=w_send, dst_ref=w_recv.at[index], send_sem=sems.at[0], recv_sem=sems.at[1],
-            device_id=(grp, chip * 2 + near), device_id_type=MESH,
-        ).start()
-
-    @pl.loop(1, CHIPS)
-    def _(step):
-        pltpu.make_async_remote_copy(
-            src_ref=w_send, dst_ref=w_recv.at[index], send_sem=sems.at[0], recv_sem=sems.at[1],
-            device_id=(grp, lax.rem(chip + step, CHIPS) * 2 + near), device_id_type=MESH,
-        ).start()
 
     def all_blocks_m(step):
         peer = member(step)
@@ -190,9 +209,13 @@
 
     pltpu.make_async_copy(send_m.at[trn], recv_m.at[trn], sems.at[5]).start()
     pl.loop(1, MEMBERS)(all_blocks_m)
-    exchange(send_a, recv_a, 16, 2, 3)
-
-    arrived(w_recv, 1)
+
+    copies_in[6].wait()
+    send[2] = pack(dot(order[...], cot[...]))
+    exchange(2)
+    restore[...] = jnp.where(pos_col == iota((R, R), 1), 1.0, 0.0).astype(BF16)
+
+    wait_for(w_recv, 1)
     for step in range(CHIPS):
         w_rows[2 * step : 2 * step + 2, :] = w_recv[step]
     w_full[grp, core] = w_rows[...].astype(BF16)
@@ -236,6 +259,7 @@
     swap_w.wait()
 
     weight = w_full[...].reshape(D, HD)
+    copies_in[7].wait()
     vals[...] = dot(feat[...], weight).astype(BF16)
 
     def attend(p_ref, v_ref, out_ref):
@@ -272,10 +296,10 @@
             dk_ref[cols(pair)] = (jnp.where(low_lane, dk[0], dk[1]) * factor).astype(dk_ref.dtype)
 
     attend(stop_p, vals, ctx)
-    send_c[...] = pack(dot(order[...], ctx[...]))
-    exchange(send_c, recv_c, 16, 10, 11)
-
-    arrived(recv_m, 5)
+    send[3] = pack(dot(order[...], ctx[...]))
+    exchange(3)
+
+    wait_for(recv_m, 5)
     got = jnp.broadcast_to(recv_m[...], (MEMBERS, 8, 128)).reshape(R, 128)
 
     def field(number):
@@ -285,29 +309,33 @@
     buckets = field(2)
     allowed = (piece == to_row(piece)) & (to_row(buckets) <= buckets)
     bias[...] = jnp.where(allowed, 0.0, NEG)
-    arrived(recv_a, 3)
-    qw[...] = unpack(recv_a[:, 0:half])
-    kw[...] = unpack(recv_a[:, half : 2 * half])
-    dw[...] = unpack(recv_a[:, 2 * half :])
+    arrived(0)
+    qw[...] = unpack(recv[0])
+    arrived(1)
+    kw[...] = unpack(recv[1])
     weights_into(win_p, qw, kw)
+    arrived(2)
+    dw[...] = unpack(recv[2])
     attend_value_back(win_p, dw, out_m)
-    send_d[...] = pack(out_m[...])
-    exchange(send_d, recv_d, 16, 12, 13)
-
-    arrived(recv_c, 11)
-    vw[...] = unpack(recv_c[...])
+    send[4] = pack(out_m[...])
+    exchange(4)
+
+    arrived(3)
+    vw[...] = unpack(recv[3])
     attend(win_p, vw, out_m)
+    send[5] = pack(out_m[...])
+    exchange(5)
     attend_back(win_p, qw, kw, vw, dw, out_q, out_k)
-    send_r[:, 0:half] = pack(out_m[...])
-    send_r[:, half : 2 * half] = pack(out_q[...])
-    send_r[:, 2 * half :] = pack(out_k[...])
-    exchange(send_r, recv_r, 16, 14, 15)
-
-    def put_back(block):
-        return dot(restore[...], unpack(block))
-
-    arrived(recv_d, 13)
-    grad_c[...] = put_back(recv_d[...]).astype(BF16)
+    send[6] = pack(out_q[...])
+    exchange(6)
+    send[7] = pack(out_k[...])
+    exchange(7)
+
+    def put_back(number):
+        arrived(number)
+        return dot(restore[...], unpack(recv[number]))
+
+    grad_c[...] = put_back(4).astype(BF16)
     attend_value_back(stop_p, grad_c, grad_v)
 
     mine = (slice(None), pl.ds(pl.multiple_of(core * half, half), half))
@@ -337,49 +365,85 @@
     total = rs1_recv[0].astype(F32)
     for step in range(1, GROUPS):
         total = total + rs1_recv[step].astype(F32)
-    for step in range(CHIPS):
-        rs2_send[step] = total[4 * step : 4 * step + 4]
-    rs2_recv[chip] = rs2_send[chip]
-
-    @pl.loop(1, CHIPS)
+    rs1_sum[...] = total
+
+    swap_2 = pltpu.make_async_remote_copy(
+        src_ref=rs1_sum.at[pl.ds(pl.multiple_of(32 * (1 - core), 32), 32)], dst_ref=rs2_swap,
+        send_sem=sems.at[20], recv_sem=sems.at[21], device_id=(grp, sibling), device_id_type=MESH,
+    )
+    swap_2.start()
+    gfeat_o[...] = dot_nt(grad_v[...], w_full[...].reshape(D, HD)).astype(BF16)
+    swap_2.wait()
+    is_first = core == 0
+    kept = rs1_sum[pl.ds(pl.multiple_of(32 * core, 32), 32), :]
+    swapped = rs2_swap[...]
+    sides = (jnp.where(is_first, kept, swapped), jnp.where(is_first, swapped, kept))
+    for step in range(CHIPS // 2):
+        for part in range(4):
+            piece_4 = sides[part // 2][4 * step : 4 * step + 4, 128 * (part % 2) : 128 * (part % 2) + 128]
+            rs2_rows[16 * step + 4 * part : 16 * step + 4 * part + 4, :] = piece_4
+    rs2_send[...] = rs2_rows[...].astype(BF16)
+
+    def part_16(ref, who):
+        return ref.at[pl.ds(pl.multiple_of(who * 16, 16), 16)]
+
+    eight = lax.rem(chip, 8)
+    summing = core == chip // 8
+
+    @pl.when(summing)
+    def _():
+        pltpu.make_async_copy(part_16(rs2_send, eight), part_16(rs2_recv, chip), sems.at[23]).start()
+
+    @pl.when(jnp.logical_not(summing))
+    def _():
+        pltpu.make_async_remote_copy(
+            src_ref=part_16(rs2_send, eight), dst_ref=part_16(rs2_recv, chip),
+            send_sem=sems.at[22], recv_sem=sems.at[23],
+            device_id=(grp, (8 * core + eight) * 2 + core), device_id_type=MESH,
+        ).start()
+
+    @pl.loop(1, 8)
     def _(step):
-        peer = lax.rem(chip + step, CHIPS)
-        pltpu.make_async_remote_copy(
-            src_ref=rs2_send.at[peer], dst_ref=rs2_recv.at[chip], send_sem=sems.at[20], recv_sem=sems.at[21],
-            device_id=(grp, peer * 2 + core), device_id_type=MESH,
-        ).start()
-
-    gfeat_o[...] = dot_nt(grad_v[...], w_full[...].reshape(D, HD)).astype(BF16)
-
-    wait_for(rs2_recv.at[pl.ds(0, CHIPS - 1)], 21)
-    mine_4 = rs2_recv[0]
-    for step in range(1, CHIPS):
-        mine_4 = mine_4 + rs2_recv[step]
-    mine_4 = mine_4 * ((R * MEMBERS * GROUPS) ** -0.5)
-    first, second = mine_4[0:2], mine_4[2:4]
-    is_first = core == 0
-    rs3_send[...] = jnp.where(is_first, second, first)
-    swap_3 = pltpu.make_async_remote_copy(
-        src_ref=rs3_send, dst_ref=rs3_recv, send_sem=sems.at[22], recv_sem=sems.at[23],
+        peer = lax.rem(eight + step, 8)
+        pltpu.make_async_remote_copy(
+            src_ref=part_16(rs2_send, peer), dst_ref=part_16(rs2_recv, chip),
+            send_sem=sems.at[22], recv_sem=sems.at[23],
+            device_id=(grp, (8 * core + peer) * 2 + core), device_id_type=MESH,
+        ).start()
+
+    mixed_o[...] = put_back(5).astype(BF16)
+    gq_o[...] = (stop_q[...] + put_back(6)).astype(BF16)
+
+    give = pltpu.make_async_remote_copy(
+        src_ref=rs3_send, dst_ref=rs3_recv, send_sem=sems.at[2], recv_sem=sems.at[3],
         device_id=(grp, sibling), device_id_type=MESH,
     )
-    swap_3.start()
-    kept = jnp.where(is_first, first, second)
-    swap_3.wait()
-    swapped = rs3_recv[...]
-    gw_o[:, 0:half] = jnp.where(is_first, kept, swapped)
-    gw_o[:, half:] = jnp.where(is_first, swapped, kept)
-
-    arrived(recv_r, 15)
-    mixed_o[...] = put_back(recv_r[:, 0:half]).astype(BF16)
-    gq_o[...] = (stop_q[...] + put_back(recv_r[:, half : 2 * half])).astype(BF16)
-    gk_o[...] = (stop_k[...] + put_back(recv_r[:, 2 * half :])).astype(BF16)
-
-    sent(send_a, 16, 2)
-    sent(send_m, 1, 4)
-    sent(send_c, 16, 10)
-    sent(send_d, 16, 12)
-    sent(send_r, 16, 14)
+
+    @pl.when(summing)
+    def _():
+        wait_for(rs2_recv, 23)
+        rows_16 = jnp.sum(rs2_recv[...].astype(F32).reshape(CHIPS, 16, 128), axis=0)
+        rs3_rows[...] = rows_16 * ((R * MEMBERS * GROUPS) ** -0.5)
+        four = [rs3_rows[4 * part : 4 * part + 4, :] for part in range(4)]
+        rows_4 = jnp.concatenate(four, axis=1)
+        rs3_send[...] = jnp.where(is_first, rows_4[2:4], rows_4[0:2])
+        give.start()
+        gw_o[...] = jnp.where(is_first, rows_4[0:2], rows_4[2:4])
+
+    gk_o[...] = (stop_k[...] + put_back(7)).astype(BF16)
+
+    @pl.when(summing)
+    def _():
+        give.wait_send()
+
+    @pl.when(jnp.logical_not(summing))
+    def _():
+        give.wait_recv()
+        gw_o[...] = rs3_recv[...]
+
+    for number in range(8):
+        sent(number)
+    wait_for(send_m.at[pl.ds(0, MEMBERS - 1)], 4)
     wait_for(w_recv.at[pl.ds(0, CHIPS - 1)], 0)
 
     @pl.when(jnp.logical_not(own_near))
@@ -387,7 +451,23 @@
         wait_for(w_send, 0)
 
     wait_for(rs1_send.at[pl.ds(0, GROUPS - 1)], 18)
-    wait_for(rs2_send.at[pl.ds(0, CHIPS - 1)], 20)
+    wait_for(rs2_send.at[pl.ds(0, 7 * 16)], 22)
+
+    @pl.when(jnp.logical_not(summing))
+    def _():
+        wait_for(rs2_send.at[pl.ds(0, 16)], 22)
+
+
+def write(*refs):
+    *pairs, sems = refs
+    copies = [
+        pltpu.make_async_copy(source, target, sems.at[number])
+        for number, (source, target) in enumerate(zip(pairs[:5], pairs[5:]))
+    ]
+    for copy in copies:
+        copy.start()
+    for copy in copies:
+        copy.wait()
 
 
 def shards(features, query_rows, key_rows, w_value, cotangent, station, bucket, slot_index):
@@ -398,13 +478,12 @@
         return pltpu.VMEM(shape, dtype)
 
     scratch = [
+        buffer((R, D), BF16), buffer((R, HD), BF16), buffer((R, HD), BF16), buffer((2, HD), BF16), buffer((R, HD), BF16),
+        buffer((1, R), I32), buffer((1, R), I32), buffer((1, R), I32),
         buffer((R, R), BF16), buffer((R, R), BF16), buffer((R, R), F32),
         buffer((HEADS, R, R), BF16), buffer((HEADS, R, R), BF16),
-        buffer((2 * R, 3 * half), BF16), buffer((2 * R, 3 * half), BF16),
+        buffer((8, 2 * R, half), BF16), buffer((8, 2 * R, half), BF16),
         buffer((MEMBERS, 1, 128), I32), buffer((MEMBERS, 1, 128), I32),
-        buffer((2 * R, half), BF16), buffer((2 * R, half), BF16),
-        buffer((2 * R, half), BF16), buffer((2 * R, half), BF16),
-        buffer((2 * R, 3 * half), BF16), buffer((2 * R, 3 * half), BF16),
         buffer((2, HD), F32), buffer((CHIPS, 2, HD), F32), buffer((32, HD), F32), buffer((GROUPS, 2, 32, HD), BF16),
         buffer((R, HD), BF16), buffer((R, HD), BF16), buffer((R, HD), BF16), buffer((R, HD), BF16),
         buffer((R, HD), F32), buffer((R, HD), F32),
@@ -412,30 +491,35 @@
         buffer((R, HD), F32), buffer((R, HD), F32), buffer((R, HD), F32),
         buffer((D, half), F32), buffer((D, half), BF16), buffer((D, half), BF16),
         buffer((GROUPS, 64, half), BF16), buffer((GROUPS, 64, half), BF16),
-        buffer((CHIPS, 4, half), F32), buffer((CHIPS, 4, half), F32),
-        buffer((2, half), F32), buffer((2, half), F32),
-        pltpu.SemaphoreType.DMA((24,)),
+        buffer((64, half), F32), buffer((32, half), F32), buffer((128, 128), F32), buffer((128, 128), BF16),
+        buffer((R, 128), BF16), buffer((16, 128), F32), buffer((2, HD), F32), buffer((2, HD), F32),
+        pltpu.SemaphoreType.DMA((24,)), pltpu.SemaphoreType.DMA((8,)),
+        pltpu.SemaphoreType.DMA((8,)), pltpu.SemaphoreType.DMA((8,)),
     ]
-    return pl.pallas_call(
+    kinds = (((R, HD), BF16), ((R, D), BF16), ((R, HD), BF16), ((R, HD), BF16), ((2, HD), F32))
+    inputs = (
+        features, query_rows, key_rows, w_value, cotangent,
+        station.reshape(1, R), bucket.reshape(1, R), slot_index.reshape(1, R),
+    )
+    results = pl.pallas_call(
         kernel,
-        out_shape=(
-            jax.ShapeDtypeStruct((R, HD), BF16),
-            jax.ShapeDtypeStruct((R, D), BF16),
-            jax.ShapeDtypeStruct((R, HD), BF16),
-            jax.ShapeDtypeStruct((R, HD), BF16),
-            jax.ShapeDtypeStruct((2, HD), F32),
-        ),
-        in_specs=[vmem] * 8,
+        out_shape=tuple(pltpu.VMEM(*kind) for kind in kinds),
+        in_specs=[pl.BlockSpec(memory_space=pltpu.HBM)] * 8,
         out_specs=(vmem,) * 5,
         scratch_shapes=scratch,
         compiler_params=pltpu.CompilerParams(
             collective_id=0, has_side_effects=True, vmem_limit_bytes=48 * 1024 * 1024
         ),
         name="delay_attention",
-    )(
-        features, query_rows, key_rows, w_value, cotangent,
-        station.reshape(1, R), bucket.reshape(1, R), slot_index.reshape(1, R),
-    )
+    )(*(pltpu.with_memory_space_constraint(array, pltpu.HBM) for array in inputs))
+    return pl.pallas_call(
+        write,
+        out_shape=tuple(jax.ShapeDtypeStruct(*kind) for kind in kinds),
+        in_specs=[vmem] * 5,
+        out_specs=(pl.BlockSpec(memory_space=pltpu.HBM),) * 5,
+        scratch_shapes=[pltpu.SemaphoreType.DMA((5,))],
+        name="write_results",
+    )(*(pltpu.with_memory_space_constraint(array, pltpu.VMEM) for array in results))
 
 
 def solution(mesh):

time: 128 us -> 120 us (0.938)
  local copies, waits for them, and re-layouts: 8.08 us -> 0 us
    unnamed x21 -> x0, local copies, waits for them, and re-layouts: 8.08 us -> none
    pallas_call x1 -> x2, Pallas kernels: 119 us -> 119 us  [the longest x1 118 us: shards(): pl.pallas_call(kernel, out_shape=tuple((pltpu.VMEM(*kind) for kind in kin...]
where the time goes in v2:
time: 120 us
  Pallas kernels  119 us (99%)
    pallas_call x1, Pallas kernels, shards(): pl.pallas_call(kernel, out_shape=tuple((pltpu.VMEM(*kind) for kind in kin...  118 us

profile of v2, /device:TPU:1, one launch (start us, length us, event | category | flops | bytes accessed | tf_op | source)
XLA Modules:
  0.0 119.9 jit_solution(8595529003550255693)
XLA Ops:
  0.6 118.1 %delay_attention.1 = (bf16[256,512]{1,0:T(8,128)(2,1)S(1)}, bf16[256,1024]{1,0:T(8,128)(2,1)S(1)}, bf16[256,512]{1,0:T(8,128)(2,1)S(1)}, bf16[256,512]{1,0:T(8,128)(2,1)S(1)}, f32[2,512]{1,0:T(2,128)S(1)}) custom-call(bf16[256,1024]{1,0:T(8,128)(2,1)} %feat_in.1, bf16[256,512]{1,0:T(8,128)(2,1)} %query_in.1, bf16[256,512]{1,0:T(8,128)(2,1)} %key_in.1, ...), custom_call_target="tpu_custom_call" | custom-call | tf_op jit(solution)/shard_map/delay_attention/pallas_call | solution.py:504
  118.8 1.1 write_results.1

commit v3 on v2

--- a/solution.py
+++ b/solution.py
@@ -73,7 +73,7 @@
     feat, query, key, w_part, cot, station, bucket, slot,
     order, restore, bias, stop_p, win_p,
     send, recv, send_m, recv_m,
-    w_send, w_recv, w_rows, w_full,
+    w_pair, w_block, w_send, w_recv, w_rows, w_full,
     vals, ctx, grad_c, grad_v, stop_q, stop_k,
     qw, kw, vw, dw, out_m, out_q, out_k,
     gw_own, rs0_send, rs0_recv, rs1_send, rs1_recv, rs1_sum, rs2_swap, rs2_rows, rs2_send, rs2_recv,
@@ -114,10 +114,11 @@
     def block(number, ref, who):
         return ref.at[number, pl.ds(pl.multiple_of(who * 16, 16), 16)]
 
-    def exchange(number):
-        pltpu.make_async_copy(block(number, send, trn), block(number, recv, trn), recv_sems.at[number]).start()
-
-        @pl.loop(1, MEMBERS)
+    def exchange(number, first=1, last=MEMBERS):
+        if first == 1:
+            pltpu.make_async_copy(block(number, send, trn), block(number, recv, trn), recv_sems.at[number]).start()
+
+        @pl.loop(first, last)
         def _(step):
             peer = member(step)
             pltpu.make_async_remote_copy(
@@ -151,33 +152,44 @@
     copies_in[1].wait()
     send[0] = pack(dot(order[...], query[...]))
     copies_in[2].wait()
-    w_send[...] = w_part[...].astype(F32)
+    w_pair[core] = w_part[...].astype(F32)
 
     pl.semaphore_wait(barrier, MEMBERS - 1 + GROUPS - 1)
 
-    near = trn // 16
-    index = lax.rem(trn, 16)
-    own_near = core == near
-
-    @pl.when(own_near)
-    def _():
-        pltpu.make_async_copy(w_send, w_recv.at[index], sems.at[1]).start()
-
-    @pl.when(jnp.logical_not(own_near))
-    def _():
+    share = pltpu.make_async_remote_copy(
+        src_ref=w_pair.at[core], dst_ref=w_pair.at[core], send_sem=sems.at[0], recv_sem=sems.at[1],
+        device_id=(grp, sibling), device_id_type=MESH,
+    )
+    share.start()
+    exchange(0, 1, 9)
+    share.wait()
+    four_rows = w_pair[...].reshape(4, HD)
+    for part in range(4):
+        w_block[4 * part : 4 * part + 4, :] = four_rows[:, 128 * part : 128 * part + 128]
+    w_send[...] = w_block[...].astype(BF16)
+    near = chip // 8
+    eight = lax.rem(chip, 8)
+
+    def part_16(ref, who):
+        return ref.at[pl.ds(pl.multiple_of(who * 16, 16), 16)]
+
+    @pl.when(core == near)
+    def _():
+        pltpu.make_async_copy(w_send, part_16(w_recv, eight), sems.at[9]).start()
+
+    def send_weights(away):
         pltpu.make_async_remote_copy(
-            src_ref=w_send, dst_ref=w_recv.at[index], send_sem=sems.at[0], recv_sem=sems.at[1],
-            device_id=(grp, chip * 2 + near), device_id_type=MESH,
+            src_ref=w_send, dst_ref=part_16(w_recv, eight), send_sem=sems.at[8], recv_sem=sems.at[9],
+            device_id=(grp, lax.rem(chip + CHIPS + away, CHIPS) * 2 + near), device_id_type=MESH,
         ).start()
 
-    @pl.loop(1, CHIPS)
-    def _(step):
-        pltpu.make_async_remote_copy(
-            src_ref=w_send, dst_ref=w_recv.at[index], send_sem=sems.at[0], recv_sem=sems.at[1],
-            device_id=(grp, lax.rem(chip + step, CHIPS) * 2 + near), device_id_type=MESH,
-        ).start()
-
-    exchange(0)
+    pl.loop(1, 8)(lambda step: send_weights(step * (1 - 2 * core)))
+
+    @pl.when(core == 0)
+    def _():
+        send_weights(8)
+
+    exchange(0, 9)
     copies_in[5].wait()
     send[1] = pack(dot(order[...], key[...]))
     exchange(1)
@@ -215,9 +227,12 @@
     exchange(2)
     restore[...] = jnp.where(pos_col == iota((R, R), 1), 1.0, 0.0).astype(BF16)
 
-    wait_for(w_recv, 1)
-    for step in range(CHIPS):
-        w_rows[2 * step : 2 * step + 2, :] = w_recv[step]
+    wait_for(w_recv, 9)
+    wide = w_recv[...].astype(F32)
+    for step in range(8):
+        for part in range(4):
+            first_row = 16 * step + 4 * part
+            w_rows[4 * step : 4 * step + 4, 128 * part : 128 * part + 128] = wide[first_row : first_row + 4]
     w_full[grp, core] = w_rows[...].astype(BF16)
 
     @pl.loop(1, GROUPS)
@@ -252,7 +267,7 @@
     wait_for(w_full.at[pl.ds(0, GROUPS - 1), core], 7)
     wait_for(w_full.at[pl.ds(0, GROUPS - 1), core], 6)
     swap_w = pltpu.make_async_remote_copy(
-        src_ref=w_full.at[:, core], dst_ref=w_full.at[:, core], send_sem=sems.at[8], recv_sem=sems.at[9],
+        src_ref=w_full.at[:, core], dst_ref=w_full.at[:, core], send_sem=sems.at[10], recv_sem=sems.at[11],
         device_id=(grp, sibling), device_id_type=MESH,
     )
     swap_w.start()
@@ -329,7 +344,6 @@
     send[6] = pack(out_q[...])
     exchange(6)
     send[7] = pack(out_k[...])
-    exchange(7)
 
     def put_back(number):
         arrived(number)
@@ -384,11 +398,7 @@
             rs2_rows[16 * step + 4 * part : 16 * step + 4 * part + 4, :] = piece_4
     rs2_send[...] = rs2_rows[...].astype(BF16)
 
-    def part_16(ref, who):
-        return ref.at[pl.ds(pl.multiple_of(who * 16, 16), 16)]
-
-    eight = lax.rem(chip, 8)
-    summing = core == chip // 8
+    summing = core == near
 
     @pl.when(summing)
     def _():
@@ -411,6 +421,8 @@
             device_id=(grp, (8 * core + peer) * 2 + core), device_id_type=MESH,
         ).start()
 
+    exchange(7)
+
     mixed_o[...] = put_back(5).astype(BF16)
     gq_o[...] = (stop_q[...] + put_back(6)).astype(BF16)
 
@@ -444,11 +456,11 @@
     for number in range(8):
         sent(number)
     wait_for(send_m.at[pl.ds(0, MEMBERS - 1)], 4)
-    wait_for(w_recv.at[pl.ds(0, CHIPS - 1)], 0)
-
-    @pl.when(jnp.logical_not(own_near))
-    def _():
-        wait_for(w_send, 0)
+    wait_for(w_recv.at[pl.ds(0, 7 * 16)], 8)
+
+    @pl.when(core == 0)
+    def _():
+        wait_for(w_send, 8)
 
     wait_for(rs1_send.at[pl.ds(0, GROUPS - 1)], 18)
     wait_for(rs2_send.at[pl.ds(0, 7 * 16)], 22)
@@ -484,7 +496,8 @@
         buffer((HEADS, R, R), BF16), buffer((HEADS, R, R), BF16),
         buffer((8, 2 * R, half), BF16), buffer((8, 2 * R, half), BF16),
         buffer((MEMBERS, 1, 128), I32), buffer((MEMBERS, 1, 128), I32),
-        buffer((2, HD), F32), buffer((CHIPS, 2, HD), F32), buffer((32, HD), F32), buffer((GROUPS, 2, 32, HD), BF16),
+        buffer((2, 2, HD), F32), buffer((16, 128), F32), buffer((16, 128), BF16), buffer((128, 128), BF16),
+        buffer((32, HD), F32), buffer((GROUPS, 2, 32, HD), BF16),
         buffer((R, HD), BF16), buffer((R, HD), BF16), buffer((R, HD), BF16), buffer((R, HD), BF16),
         buffer((R, HD), F32), buffer((R, HD), F32),
         buffer((R, HD), BF16), buffer((R, HD), BF16), buffer((R, HD), BF16), buffer((R, HD), BF16),

time: 120 us -> 116 us (0.967)
  Pallas kernels: 119 us -> 115 us
    pallas_call x1, Pallas kernels: 118 us -> 114 us  [shards(): pl.pallas_call(kernel, out_shape=tuple((pltpu.VMEM(*kind) for kind in kin...]
where the time goes in v3:
time: 116 us
  Pallas kernels  115 us (99%)
    pallas_call x1, Pallas kernels, shards(): pl.pallas_call(kernel, out_shape=tuple((pltpu.VMEM(*kind) for kind in kin...  114 us

profile of v3, /device:TPU:1, one launch (start us, length us, event | category | flops | bytes accessed | tf_op | source)
XLA Modules:
  0.0 115.9 jit_solution(3385763231300914649)
XLA Ops:
  0.6 114.2 %delay_attention.1 = (bf16[256,512]{1,0:T(8,128)(2,1)S(1)}, bf16[256,1024]{1,0:T(8,128)(2,1)S(1)}, bf16[256,512]{1,0:T(8,128)(2,1)S(1)}, bf16[256,512]{1,0:T(8,128)(2,1)S(1)}, f32[2,512]{1,0:T(2,128)S(1)}) custom-call(bf16[256,1024]{1,0:T(8,128)(2,1)} %feat_in.1, bf16[256,512]{1,0:T(8,128)(2,1)} %query_in.1, bf16[256,512]{1,0:T(8,128)(2,1)} %key_in.1, ...), custom_call_target="tpu_custom_call" | custom-call | tf_op jit(solution)/shard_map/delay_attention/pallas_call | solution.py:517
  114.8 1.1 write_results.1

commit v4 on v3

--- a/solution.py
+++ b/solution.py
@@ -78,7 +78,7 @@
     qw, kw, vw, dw, out_m, out_q, out_k,
     gw_own, rs0_send, rs0_recv, rs1_send, rs1_recv, rs1_sum, rs2_swap, rs2_rows, rs2_send, rs2_recv,
     rs3_rows, rs3_send, rs3_recv,
-    sems, in_sems, send_sems, recv_sems,
+    sems, in_sems, send_sems, recv_sems, ready,
 ):
     copies_in = [
         pltpu.make_async_copy(source, target, in_sems.at[number])
@@ -87,8 +87,8 @@
             (key_in, key), (cot_in, cot), (feat_in, feat),
         ))
     ]
-    for copy in copies_in:
-        copy.start()
+    copies_in[0].start()
+    copies_in[1].start()
     grp = lax.axis_index("grp")
     trn = lax.axis_index("trn")
     chip = trn // 2
@@ -103,22 +103,38 @@
 
     barrier = pltpu.get_barrier_semaphore()
 
-    @pl.loop(1, MEMBERS)
-    def _(step):
-        pl.semaphore_signal(barrier, inc=1, device_id=(grp, member(step)), device_id_type=MESH)
-
-    @pl.loop(1, GROUPS)
-    def _(step):
-        pl.semaphore_signal(barrier, inc=1, device_id=(group(step), trn), device_id_type=MESH)
+    def greet(group_index, member_index):
+        pl.semaphore_signal(barrier, inc=1, device_id=(group_index, member_index), device_id_type=MESH)
+
+    pl.loop(1, CHIPS)(lambda step: greet(grp, lax.rem(chip + step, CHIPS) * 2))
+
+    @pl.when(core == 1)
+    def _():
+        greet(grp, sibling)
+
+    pl.loop(1, GROUPS)(lambda step: greet(group(step), chip * 2 + 1))
+
+    for copy in copies_in[2:]:
+        copy.start()
+
+    def all_in(first_core, count, number):
+        @pl.when(core == first_core)
+        def _():
+            pl.semaphore_wait(barrier, count)
+            pl.semaphore_signal(ready.at[number], inc=1, device_id=(grp, sibling), device_id_type=MESH)
+
+        @pl.when(core != first_core)
+        def _():
+            pl.semaphore_wait(ready.at[number], 1)
 
     def block(number, ref, who):
         return ref.at[number, pl.ds(pl.multiple_of(who * 16, 16), 16)]
 
-    def exchange(number, first=1, last=MEMBERS):
+    def exchange(number, first=1, stride=1):
         if first == 1:
             pltpu.make_async_copy(block(number, send, trn), block(number, recv, trn), recv_sems.at[number]).start()
 
-        @pl.loop(first, last)
+        @pl.loop(first, MEMBERS, step=stride)
         def _(step):
             peer = member(step)
             pltpu.make_async_remote_copy(
@@ -154,14 +170,14 @@
     copies_in[2].wait()
     w_pair[core] = w_part[...].astype(F32)
 
-    pl.semaphore_wait(barrier, MEMBERS - 1 + GROUPS - 1)
+    all_in(0, MEMBERS - 1, 0)
 
     share = pltpu.make_async_remote_copy(
         src_ref=w_pair.at[core], dst_ref=w_pair.at[core], send_sem=sems.at[0], recv_sem=sems.at[1],
         device_id=(grp, sibling), device_id_type=MESH,
     )
     share.start()
-    exchange(0, 1, 9)
+    exchange(0, 1, 2)
     share.wait()
     four_rows = w_pair[...].reshape(4, HD)
     for part in range(4):
@@ -189,7 +205,7 @@
     def _():
         send_weights(8)
 
-    exchange(0, 9)
+    exchange(0, 2, 2)
     copies_in[5].wait()
     send[1] = pack(dot(order[...], key[...]))
     exchange(1)
@@ -234,6 +250,7 @@
             first_row = 16 * step + 4 * part
             w_rows[4 * step : 4 * step + 4, 128 * part : 128 * part + 128] = wide[first_row : first_row + 4]
     w_full[grp, core] = w_rows[...].astype(BF16)
+    all_in(1, 2 * (GROUPS - 1), 1)
 
     @pl.loop(1, GROUPS)
     def _(step):
@@ -373,6 +390,7 @@
             device_id=(peer, trn), device_id_type=MESH,
         ).start()
 
+    exchange(7, 1, 2)
     attend_back(stop_p, query, key, vals, grad_c, stop_q, stop_k)
 
     wait_for(rs1_recv.at[pl.ds(0, GROUPS - 1)], 19)
@@ -421,7 +439,7 @@
             device_id=(grp, (8 * core + peer) * 2 + core), device_id_type=MESH,
         ).start()
 
-    exchange(7)
+    exchange(7, 2, 2)
 
     mixed_o[...] = put_back(5).astype(BF16)
     gq_o[...] = (stop_q[...] + put_back(6)).astype(BF16)
@@ -507,7 +525,7 @@
         buffer((64, half), F32), buffer((32, half), F32), buffer((128, 128), F32), buffer((128, 128), BF16),
         buffer((R, 128), BF16), buffer((16, 128), F32), buffer((2, HD), F32), buffer((2, HD), F32),
         pltpu.SemaphoreType.DMA((24,)), pltpu.SemaphoreType.DMA((8,)),
-        pltpu.SemaphoreType.DMA((8,)), pltpu.SemaphoreType.DMA((8,)),
+        pltpu.SemaphoreType.DMA((8,)), pltpu.SemaphoreType.DMA((8,)), pltpu.SemaphoreType.REGULAR((2,)),
     ]
     kinds = (((R, HD), BF16), ((R, D), BF16), ((R, HD), BF16), ((R, HD), BF16), ((2, HD), F32))
     inputs = (

time: 116 us -> 115 us (level)
    pallas_call x1, Pallas kernels: 114 us -> 113 us  [shards(): pl.pallas_call(kernel, out_shape=tuple((pltpu.VMEM(*kind) for kind in kin...]
where the time goes in v4:
time: 115 us; the launch traced here: 114 us
  Pallas kernels  114 us (99%)
    pallas_call x1, Pallas kernels, shards(): pl.pallas_call(kernel, out_shape=tuple((pltpu.VMEM(*kind) for kind in kin...  113 us

profile of v4, /device:TPU:1, one launch (start us, length us, event | category | flops | bytes accessed | tf_op | source)
XLA Modules:
  0.0 114.4 jit_solution(17716517332666715100)
XLA Ops:
  0.6 112.6 %delay_attention.1 = (bf16[256,512]{1,0:T(8,128)(2,1)S(1)}, bf16[256,1024]{1,0:T(8,128)(2,1)S(1)}, bf16[256,512]{1,0:T(8,128)(2,1)S(1)}, bf16[256,512]{1,0:T(8,128)(2,1)S(1)}, f32[2,512]{1,0:T(2,128)S(1)}) custom-call(bf16[256,1024]{1,0:T(8,128)(2,1)} %feat_in.1, bf16[256,512]{1,0:T(8,128)(2,1)} %query_in.1, bf16[256,512]{1,0:T(8,128)(2,1)} %key_in.1, ...), custom_call_target="tpu_custom_call" | custom-call | tf_op jit(solution)/shard_map/delay_attention/pallas_call | solution.py:535
  113.3 1.1 write_results.1

commit v5 on v4

--- a/solution.py
+++ b/solution.py
@@ -112,8 +112,6 @@
     def _():
         greet(grp, sibling)
 
-    pl.loop(1, GROUPS)(lambda step: greet(group(step), chip * 2 + 1))
-
     for copy in copies_in[2:]:
         copy.start()
 
@@ -189,23 +187,38 @@
     def part_16(ref, who):
         return ref.at[pl.ds(pl.multiple_of(who * 16, 16), 16)]
 
+    high, low = eight // 4, lax.rem(chip, 4)
+
     @pl.when(core == near)
     def _():
-        pltpu.make_async_copy(w_send, part_16(w_recv, eight), sems.at[9]).start()
+        pltpu.make_async_copy(w_send, w_recv.at[high, low], sems.at[9]).start()
 
     def send_weights(away):
         pltpu.make_async_remote_copy(
-            src_ref=w_send, dst_ref=part_16(w_recv, eight), send_sem=sems.at[8], recv_sem=sems.at[9],
+            src_ref=w_send, dst_ref=w_recv.at[high, low], send_sem=sems.at[8], recv_sem=sems.at[9],
             device_id=(grp, lax.rem(chip + CHIPS + away, CHIPS) * 2 + near), device_id_type=MESH,
         ).start()
 
-    pl.loop(1, 8)(lambda step: send_weights(step * (1 - 2 * core)))
+    send_weights(4 - 8 * core)
 
     @pl.when(core == 0)
     def _():
         send_weights(8)
 
     exchange(0, 2, 2)
+
+    wait_for(w_recv.at[:, low], 9)
+
+    def spread_weights(away):
+        pltpu.make_async_remote_copy(
+            src_ref=w_recv.at[:, low], dst_ref=w_recv.at[:, low], send_sem=sems.at[24], recv_sem=sems.at[25],
+            device_id=(grp, lax.rem(chip + CHIPS + away, CHIPS) * 2 + core), device_id_type=MESH,
+        ).start()
+
+    for away in (1, -1, 2 - 4 * core):
+        spread_weights(away)
+
+    pl.loop(1, GROUPS)(lambda step: greet(group(step), chip * 2 + 1))
     copies_in[5].wait()
     send[1] = pack(dot(order[...], key[...]))
     exchange(1)
@@ -243,8 +256,8 @@
     exchange(2)
     restore[...] = jnp.where(pos_col == iota((R, R), 1), 1.0, 0.0).astype(BF16)
 
-    wait_for(w_recv, 9)
-    wide = w_recv[...].astype(F32)
+    wait_for(w_recv.at[:, pl.ds(0, 3)], 25)
+    wide = w_recv[...].astype(F32).reshape(128, 128)
     for step in range(8):
         for part in range(4):
             first_row = 16 * step + 4 * part
@@ -474,12 +487,13 @@
     for number in range(8):
         sent(number)
     wait_for(send_m.at[pl.ds(0, MEMBERS - 1)], 4)
-    wait_for(w_recv.at[pl.ds(0, 7 * 16)], 8)
+    wait_for(w_send, 8)
 
     @pl.when(core == 0)
     def _():
         wait_for(w_send, 8)
 
+    wait_for(w_recv.at[:, pl.ds(0, 3)], 24)
     wait_for(rs1_send.at[pl.ds(0, GROUPS - 1)], 18)
     wait_for(rs2_send.at[pl.ds(0, 7 * 16)], 22)
 
@@ -514,7 +528,7 @@
         buffer((HEADS, R, R), BF16), buffer((HEADS, R, R), BF16),
         buffer((8, 2 * R, half), BF16), buffer((8, 2 * R, half), BF16),
         buffer((MEMBERS, 1, 128), I32), buffer((MEMBERS, 1, 128), I32),
-        buffer((2, 2, HD), F32), buffer((16, 128), F32), buffer((16, 128), BF16), buffer((128, 128), BF16),
+        buffer((2, 2, HD), F32), buffer((16, 128), F32), buffer((16, 128), BF16), buffer((2, 4, 16, 128), BF16),
         buffer((32, HD), F32), buffer((GROUPS, 2, 32, HD), BF16),
         buffer((R, HD), BF16), buffer((R, HD), BF16), buffer((R, HD), BF16), buffer((R, HD), BF16),
         buffer((R, HD), F32), buffer((R, HD), F32),
@@ -524,7 +538,7 @@
         buffer((GROUPS, 64, half), BF16), buffer((GROUPS, 64, half), BF16),
         buffer((64, half), F32), buffer((32, half), F32), buffer((128, 128), F32), buffer((128, 128), BF16),
         buffer((R, 128), BF16), buffer((16, 128), F32), buffer((2, HD), F32), buffer((2, HD), F32),
-        pltpu.SemaphoreType.DMA((24,)), pltpu.SemaphoreType.DMA((8,)),
+        pltpu.SemaphoreType.DMA((26,)), pltpu.SemaphoreType.DMA((8,)),
         pltpu.SemaphoreType.DMA((8,)), pltpu.SemaphoreType.DMA((8,)), pltpu.SemaphoreType.REGULAR((2,)),
     ]
     kinds = (((R, HD), BF16), ((R, D), BF16), ((R, HD), BF16), ((R, HD), BF16), ((2, HD), F32))

time: 115 us -> 114 us (level)
  no operation moved by 1% of the time
where the time goes in v5:
time: 114 us; the launch traced here: 113 us
  Pallas kernels  113 us (99%)
    pallas_call x1, Pallas kernels, shards(): pl.pallas_call(kernel, out_shape=tuple((pltpu.VMEM(*kind) for kind in kin...  112 us

profile of v5, /device:TPU:1, one launch (start us, length us, event | category | flops | bytes accessed | tf_op | source)
XLA Modules:
  0.0 113.5 jit_solution(13588566452353402819)
XLA Ops:
  0.6 111.7 %delay_attention.1 = (bf16[256,512]{1,0:T(8,128)(2,1)S(1)}, bf16[256,1024]{1,0:T(8,128)(2,1)S(1)}, bf16[256,512]{1,0:T(8,128)(2,1)S(1)}, bf16[256,512]{1,0:T(8,128)(2,1)S(1)}, f32[2,512]{1,0:T(2,128)S(1)}) custom-call(bf16[256,1024]{1,0:T(8,128)(2,1)} %feat_in.1, bf16[256,512]{1,0:T(8,128)(2,1)} %query_in.1, bf16[256,512]{1,0:T(8,128)(2,1)} %key_in.1, ...), custom_call_target="tpu_custom_call" | custom-call | tf_op jit(solution)/shard_map/delay_attention/pallas_call | solution.py:549
  112.4 1.1 write_results.1

commit v6 on v5

--- a/solution.py
+++ b/solution.py
@@ -417,6 +417,7 @@
         send_sem=sems.at[20], recv_sem=sems.at[21], device_id=(grp, sibling), device_id_type=MESH,
     )
     swap_2.start()
+    exchange(7, 2, 4)
     gfeat_o[...] = dot_nt(grad_v[...], w_full[...].reshape(D, HD)).astype(BF16)
     swap_2.wait()
     is_first = core == 0
@@ -452,7 +453,7 @@
             device_id=(grp, (8 * core + peer) * 2 + core), device_id_type=MESH,
         ).start()
 
-    exchange(7, 2, 2)
+    exchange(7, 4, 4)
 
     mixed_o[...] = put_back(5).astype(BF16)
     gq_o[...] = (stop_q[...] + put_back(6)).astype(BF16)

time: 114 us -> 114 us (level)
  no operation moved by 1% of the time
where the time goes in v6:
time: 114 us
  Pallas kernels  113 us (99%)
    pallas_call x1, Pallas kernels, shards(): pl.pallas_call(kernel, out_shape=tuple((pltpu.VMEM(*kind) for kind in kin...  112 us

profile of v6, /device:TPU:1, one launch (start us, length us, event | category | flops | bytes accessed | tf_op | source)
XLA Modules:
  0.0 113.6 jit_solution(5134175917293814473)
XLA Ops:
  0.6 111.8 %delay_attention.1 = (bf16[256,512]{1,0:T(8,128)(2,1)S(1)}, bf16[256,1024]{1,0:T(8,128)(2,1)S(1)}, bf16[256,512]{1,0:T(8,128)(2,1)S(1)}, bf16[256,512]{1,0:T(8,128)(2,1)S(1)}, f32[2,512]{1,0:T(2,128)S(1)}) custom-call(bf16[256,1024]{1,0:T(8,128)(2,1)} %feat_in.1, bf16[256,512]{1,0:T(8,128)(2,1)} %query_in.1, bf16[256,512]{1,0:T(8,128)(2,1)} %key_in.1, ...), custom_call_target="tpu_custom_call" | custom-call | tf_op jit(solution)/shard_map/delay_attention/pallas_call | solution.py:550
  112.5 1.1 write_results.1
